TPU v7x, 256 devices: a whole 4x4x8 slice. The times are simulated.
256 devices in a mesh: ctx: 16 (over z, core), tp: 4 (over y), dp: 4 (over x).
Axes of the slice: x: 4, y: 4, z: 8, core: 2. Of those that a mesh axis runs over, the one named last changes fastest.
Arguments:
- queries: bfloat16 [49152, 4096], P(('dp', 'ctx'), 'tp'), parts along dimension 0, may hold values from -6 to 6
- key_vectors: bfloat16 [49152, 4096], P(('dp', 'ctx'), 'tp'), parts along dimension 0, may hold values from -6 to 6
- value_vectors: bfloat16 [49152, 4096], P(('dp', 'ctx'), 'tp'), parts along dimension 0, may hold values from -6 to 6
- out_grad: bfloat16 [49152, 4096], P(('dp', 'ctx'), 'tp'), parts along dimension 0, may hold values from -6 to 6
Outputs:
- grad_queries: bfloat16 [49152, 4096], P(('dp', 'ctx'), 'tp'), parts along dimension 0
- grad_keys: bfloat16 [49152, 4096], P(('dp', 'ctx'), 'tp'), parts along dimension 0
- grad_values: bfloat16 [49152, 4096], P(('dp', 'ctx'), 'tp'), parts along dimension 0
There are 4 independent parts, one for each index of `dp`. A program takes and returns all parts, laid end to end along the dimension named above; each array names one. Nothing has to cross between parts.
All inputs are finite; a program needn't handle non-finite values.
Results may differ from a plain program's by a relative error of at most 0.014.
Values may be sent and summed in bfloat16 or wider, within the bound.
No kernel may reach another device: no remote copies, remote signals or barrier semaphores. Data moves between devices by JAX's collectives and lax.ppermute only.
A program may use at most 128 MiB of HBM per device.

v0:
```python
import math

import jax
import jax.numpy as jnp
from jax import lax
from jax.sharding import PartitionSpec as P

HEAD = 128


def head_block(query_rows, key_rows, value_rows, grad_rows, prefix_low, suffix_low, factor):
    count_rows = query_rows.shape[0]
    causal = lax.broadcasted_iota(jnp.int32, (count_rows, count_rows), 0) >= lax.broadcasted_iota(
        jnp.int32, (count_rows, count_rows), 1
    )
    scores = jnp.dot(query_rows, key_rows.T, preferred_element_type=jnp.float32)
    weights = jnp.where(causal, factor * scores, 0.0).astype(jnp.bfloat16)
    upstream = jnp.where(
        causal, factor * jnp.dot(grad_rows, value_rows.T, preferred_element_type=jnp.float32), 0.0
    ).astype(jnp.bfloat16)
    grad_query = jnp.dot(upstream, key_rows, preferred_element_type=jnp.float32) + jnp.dot(
        grad_rows, prefix_low.T, preferred_element_type=jnp.float32
    )
    grad_key = jnp.dot(upstream.T, query_rows, preferred_element_type=jnp.float32) + jnp.dot(
        value_rows, suffix_low.T, preferred_element_type=jnp.float32
    )
    grad_value = jnp.dot(weights.T, grad_rows, preferred_element_type=jnp.float32) + jnp.dot(
        key_rows, suffix_low, preferred_element_type=jnp.float32
    )
    return (
        grad_query.astype(jnp.bfloat16),
        grad_key.astype(jnp.bfloat16),
        grad_value.astype(jnp.bfloat16),
    )


def on_device(queries, key_vectors, value_vectors, out_grad):
    count_rows = queries.shape[0]
    local_heads = queries.shape[1] // HEAD
    factor = 1.0 / math.sqrt(HEAD * count_rows * lax.axis_size("ctx"))

    def heads_first(matrix_in):
        return matrix_in.reshape(count_rows, local_heads, HEAD).transpose(1, 0, 2)

    query_heads = heads_first(queries)
    key_heads = heads_first(key_vectors)
    value_heads = heads_first(value_vectors)
    grad_heads = heads_first(out_grad)
    local_state = (
        factor
        * jnp.einsum("hti,htj->hij", key_heads, value_heads, preferred_element_type=jnp.float32)
    ).astype(jnp.bfloat16)
    local_grad = (
        factor
        * jnp.einsum("hti,htj->hij", query_heads, grad_heads, preferred_element_type=jnp.float32)
    ).astype(jnp.bfloat16)
    shard_index = lax.axis_index("ctx")
    pieces = (
        lax.all_gather(local_state[None], "ctx", axis=0, tiled=True),
        lax.all_gather(local_grad[None], "ctx", axis=0, tiled=True),
    )
    count_pieces = pieces[0].shape[0]
    positions = jnp.arange(count_pieces, dtype=jnp.int32)
    earlier_mask = (positions < shard_index).astype(jnp.float32)
    later_mask = (positions > shard_index).astype(jnp.float32)
    summed_states = jnp.sum(
        earlier_mask[:, None, None, None] * pieces[0].astype(jnp.float32), axis=0
    )
    summed_grads = jnp.sum(later_mask[:, None, None, None] * pieces[1].astype(jnp.float32), axis=0)
    prefix_low = summed_states.astype(jnp.bfloat16)
    suffix_low = summed_grads.astype(jnp.bfloat16)

    def one_head(operands):
        return head_block(*operands, factor)

    grad_query, grad_key, grad_value = lax.map(
        one_head, (query_heads, key_heads, value_heads, grad_heads, prefix_low, suffix_low)
    )

    def rows_first(tensor_in):
        return tensor_in.transpose(1, 0, 2).reshape(count_rows, local_heads * HEAD)

    return (rows_first(grad_query), rows_first(grad_key), rows_first(grad_value))


def solution(mesh):
    return jax.shard_map(
        on_device,
        mesh=mesh,
        in_specs=(
            P(("dp", "ctx"), "tp"),
            P(("dp", "ctx"), "tp"),
            P(("dp", "ctx"), "tp"),
            P(("dp", "ctx"), "tp"),
        ),
        out_specs=(P(("dp", "ctx"), "tp"), P(("dp", "ctx"), "tp"), P(("dp", "ctx"), "tp")),
        check_vma=False,
    )
```

profile of v0, /device:TPU:1, one launch (start us, length us, event | category | flops | bytes accessed | tf_op | source)
XLA Modules:
  0.0 201.7 jit_solution(6657890150641122606)
XLA Ops:
  12.0 2.6 %copy.29 = bf16[768,1024]{0,1:T(8,128)(2,1)} copy(bf16[768,1024]{1,0:T(8,128)(2,1)} %param.6) | data formatting | bytes 3145728 | tf_op args[0]
  14.7 2.6 %copy.25 = bf16[768,1024]{0,1:T(8,128)(2,1)} copy(bf16[768,1024]{1,0:T(8,128)(2,1)} %param.9) | data formatting | bytes 3145728 | tf_op args[3]
  17.2 3.1 %fusion.57 = bf16[8,128,128]{2,1,0:T(8,128)(2,1)} fusion(bf16[8,768,128]{1,2,0:T(8,128)(2,1)} %bitcast.138, bf16[8,768,128]{1,2,0:T(8,128)(2,1)} %bitcast.136), kind=kOutput, calls=%fused_computation.65 | convolution fusion | flops 201588736 | bytes 3407872 | tf_op jit(solution)/shard_map/hti,htj->hij/dot_general | solution.py:55
  20.5 38.0 %all-gather.5.cloned.1.call-done = bf16[128,128,128]{2,1,0:T(8,128)(2,1)} async-done(((bf16[8,128,128]{2,1,0:T(8,128)(2,1)}), bf16[128,128,128]{2,1,0:T(8,128)(2,1)}) %all-gather.5.cloned.1.call-update) | async-done | bytes 4194320 | tf_op jit(solution)/shard_map/all_gather | solution.py:59
  58.5 3.9 %fusion.55 = bf16[8,128,128]{2,1,0:T(8,128)(2,1)} fusion(bf16[16,8,128,128]{3,2,1,0:T(8,128)(2,1)} %bitcast.140, f32[16]{0:T(128)S(1)} %get-tuple-element.101), kind=kLoop, calls=%fused_computation.58 | loop fusion | flops 6160384 | bytes 4456512 | tf_op jit(solution)/shard_map/reduce_sum | solution.py:66
  62.4 38.6 %all-gather.7.cloned.1.call-done = bf16[128,128,128]{2,1,0:T(8,128)(2,1)} async-done(((bf16[8,128,128]{2,1,0:T(8,128)(2,1)}), bf16[128,128,128]{2,1,0:T(8,128)(2,1)}) %all-gather.7.cloned.1.call-update) | async-done | bytes 4194320 | tf_op jit(solution)/shard_map/all_gather | solution.py:60
  101.0 3.9 %fusion.54 = bf16[8,128,128]{2,1,0:T(8,128)(2,1)} fusion(bf16[16,8,128,128]{3,2,1,0:T(8,128)(2,1)} %bitcast.141, f32[16]{0:T(128)S(1)} %get-tuple-element.100), kind=kLoop, calls=%fused_computation.56 | loop fusion | flops 6160384 | bytes 4456512 | tf_op jit(solution)/shard_map/reduce_sum | solution.py:69
  104.9 83.7 %while.14 = (s32[]{:T(128)}, bf16[8,768,128]{2,1,0:T(8,128)(2,1)}, bf16[8,768,128]{2,1,0:T(8,128)(2,1)}, bf16[8,768,128]{2,1,0:T(8,128)(2,1)}, bf16[8,768,128]{1...) while((s32[]{:T(128)}, bf16[8,768,128]{2,1,0:T(8,128)(2,1)}, ...), condition=%wide.region_3.4_spmd, body=%wide.region_2.3_spmd.sunk | while | flops 835780608 | bytes 8559741 | solution.py:76
  104.9 1.9 fusion.107
  110.2 1.8 fusion.104
  115.4 1.9 fusion.107
  120.6 1.8 fusion.104
  125.8 1.9 fusion.107
  131.1 1.8 fusion.104
  136.3 1.9 fusion.107
  141.6 1.8 fusion.104
  146.8 1.9 fusion.107
  152.0 1.9 fusion.104
  157.2 1.9 fusion.107
  162.5 1.8 fusion.104
  167.7 1.9 fusion.107
  172.9 1.8 fusion.104
  178.1 1.9 fusion.107
  188.6 2.9 %copy_bitcast_fusion = bf16[768,1024]{1,0:T(8,128)(2,1)} fusion(bf16[8,768,128]{2,1,0:T(8,128)(2,1)} %get-tuple-element.59), kind=kLoop, calls=%fused_computation.59 | loop fusion | bytes 3145728 | tf_op jit(solution)/shard_map/reshape | solution.py:81
  (58 shorter events, 63.5 us)
Async XLA Ops:
  7.2 51.3 %all-gather.5.cloned.1.call-start = ((), (), s32[]{:S(2)}) async-start(), calls=%async_computation | async-start | bytes 4456448 | tf_op jit(solution)/shard_map/all_gather | solution.py:59
  12.0 89.0 %all-gather.7.cloned.1.call-start = ((), (), s32[]{:S(2)}) async-start(), calls=%async_computation.1 | async-start | bytes 4456448 | tf_op jit(solution)/shard_map/all_gather | solution.py:60
  188.6 2.9 %copy-start.1 = (bf16[8,768,128]{2,1,0:T(8,128)(2,1)S(1)}, bf16[8,768,128]{2,1,0:T(8,128)(2,1)}, u32[]{:S(2)}) copy-start(bf16[8,768,128]{2,1,0:T(8,128)(2,1)} %get-tuple-element.57) | copy-start | bytes 4718596
  191.5 2.0 copy-start
Sparse Core Ops, SparseCore 0:
  12.1 46.3 all-gather.4
  60.3 40.6 all-gather.6
where the time goes:
time: 204 us; the launch traced here: 202 us
  matrix products  87.9 us (43%)
  waiting for transfers between devices  76.6 us (38%)
  local copies, waits for them, and re-layouts  14.9 us (7%)
  between operations  14.1 us (7%)
  other arithmetic  7.85 us (4%)
    all_gather x1, waiting for transfers between devices, on_device(): lax.all_gather(local_grad[None], 'ctx', axis=0, tiled=True)  38.6 us
    all_gather x1, waiting for transfers between devices, on_device(): lax.all_gather(local_state[None], 'ctx', axis=0, tiled=True)  38 us
    dot_general x8, matrix products, head_block(): jnp.dot(weights.T, grad_rows, preferred_element_type=jnp.float32)  15.2 us
    dot_general x8, matrix products, head_block(): jnp.dot(grad_rows, prefix_low.T, preferred_element_type=jnp.float32)  14.8 us
    dot_general x8, matrix products, head_block(): jnp.dot(value_rows, suffix_low.T, preferred_element_type=jnp.float32)  13.5 us
    dot_general x8, matrix products, head_block(): jnp.dot(key_rows, suffix_low, preferred_element_type=jnp.float32)  13.4 us
    dot_general x8, matrix products, head_block(): jnp.dot(upstream.T, query_rows, preferred_element_type=jnp.float32)  11.5 us
    dot_general x8, matrix products, head_block(): jnp.dot(grad_rows, value_rows.T, preferred_element_type=jnp.float32)  11.4 us
  transfers between devices with their start and end apart: 2, of which 2 were waited for; matrix products, arithmetic and copies ran while one was open for 6% of the time, Pallas kernels for 0%

commit v1 on v0

v1 whole, which is shorter than its diff:
```python
import math

import jax
import jax.numpy as jnp
from jax import lax
from jax.experimental import pallas as pl
from jax.experimental.pallas import tpu as pltpu
from jax.sharding import PartitionSpec as P

HEAD = 128
SUB = 256
PAIR = 2 * HEAD
F32 = jnp.float32
BF16 = jnp.bfloat16

NN = (((1,), (0,)), ((), ()))
NT = (((1,), (1,)), ((), ()))
TN = (((0,), (0,)), ((), ()))


def mm(a, b, dims):
    return lax.dot_general(a, b, dims, preferred_element_type=F32)


def states_kernel(factor, q_ref, k_ref, v_ref, g_ref, state_ref, local_ref):
    subs = q_ref.shape[0] // SUB
    for head in range(2):
        cols = slice(head * HEAD, (head + 1) * HEAD)
        for kind, (left, right) in enumerate(((k_ref, v_ref), (q_ref, g_ref))):
            parts = []
            for sub in range(subs):
                rows = slice(sub * SUB, (sub + 1) * SUB)
                parts.append(factor * mm(left[rows, cols], right[rows, cols], TN))
            if kind == 1:
                parts = parts[::-1]
            total = parts[0]
            for sub in range(1, subs):
                local_ref[kind, head, sub - 1] = total.astype(BF16)
                total = total + parts[sub]
            state_ref[kind, head] = total.astype(BF16)


def intra_kernel(factor, q_ref, k_ref, v_ref, g_ref, gq_ref, gk_ref, gv_ref):
    row = lax.broadcasted_iota(jnp.int32, (SUB, SUB), 0)
    col = lax.broadcasted_iota(jnp.int32, (SUB, SUB), 1)
    subs = q_ref.shape[0] // SUB
    for head in range(2):
        cols = slice(head * HEAD, (head + 1) * HEAD)
        for sub in range(subs):
            rows = slice(sub * SUB, (sub + 1) * SUB)
            q, k, v, g = (ref[rows, cols] for ref in (q_ref, k_ref, v_ref, g_ref))
            weights_t = jnp.where(col >= row, factor * mm(k, q, NT), 0.0).astype(BF16)
            upstream = jnp.where(row >= col, factor * mm(g, v, NT), 0.0).astype(BF16)
            gq_ref[rows, cols] = mm(upstream, k, NN).astype(BF16)
            gk_ref[rows, cols] = mm(upstream, q, TN).astype(BF16)
            gv_ref[rows, cols] = mm(weights_t, g, NN).astype(BF16)


def block_diagonal(first, second):
    zero = jnp.zeros_like(first)
    return jnp.concatenate(
        [jnp.concatenate([first, zero], 1), jnp.concatenate([zero, second], 1)], 0
    )


def final_kernel(
    k_ref, v_ref, g_ref, gq_in, gk_in, gv_in, prefix_ref, suffix_ref, local_ref, gq_ref, gk_ref, gv_ref
):
    subs = k_ref.shape[0] // SUB

    def of_sub(wide_ref, kind, count):
        heads = []
        for head in range(2):
            wide = wide_ref[head]
            if count > 0:
                wide = wide.astype(F32) + local_ref[kind, head, count - 1].astype(F32)
            heads.append(wide.astype(BF16))
        return block_diagonal(*heads)

    for sub in range(subs):
        rows = slice(sub * SUB, (sub + 1) * SUB)
        prefix = of_sub(prefix_ref, 0, sub)
        suffix = of_sub(suffix_ref, 1, subs - 1 - sub)
        gq_ref[rows, :] = (gq_in[rows, :].astype(F32) + mm(g_ref[rows, :], prefix, NT)).astype(BF16)
        gk_ref[rows, :] = (gk_in[rows, :].astype(F32) + mm(v_ref[rows, :], suffix, NT)).astype(BF16)
        gv_ref[rows, :] = (gv_in[rows, :].astype(F32) + mm(k_ref[rows, :], suffix, NN)).astype(BF16)


def on_device(queries, key_vectors, value_vectors, out_grad):
    rows, width = queries.shape
    heads = width // HEAD
    pairs = heads // 2
    half = heads // 2
    count_ctx = lax.axis_size("ctx")
    factor = 1.0 / math.sqrt(HEAD * rows * count_ctx)
    subs = rows // SUB
    inputs = (queries, key_vectors, value_vectors, out_grad)
    wide_spec = pl.BlockSpec((rows, PAIR), lambda p: (0, p))

    state, local = pl.pallas_call(
        lambda *refs: states_kernel(factor, *refs),
        grid=(pairs,),
        in_specs=[wide_spec] * 4,
        out_specs=(
            pl.BlockSpec((2, 2, HEAD, HEAD), lambda p: (0, p, 0, 0)),
            pl.BlockSpec((2, 2, subs - 1, HEAD, HEAD), lambda p: (0, p, 0, 0, 0)),
        ),
        out_shape=(
            jax.ShapeDtypeStruct((2, heads, HEAD, HEAD), BF16),
            jax.ShapeDtypeStruct((2, heads, subs - 1, HEAD, HEAD), BF16),
        ),
        cost_estimate=pl.CostEstimate(
            flops=4 * rows * width * HEAD, bytes_accessed=8 * rows * width, transcendentals=0
        ),
        name="states",
    )(*inputs)

    wide = jax.ShapeDtypeStruct((rows, width), BF16)
    partial = pl.pallas_call(
        lambda *refs: intra_kernel(factor, *refs),
        grid=(pairs,),
        in_specs=[wide_spec] * 4,
        out_specs=(wide_spec,) * 3,
        out_shape=(wide,) * 3,
        cost_estimate=pl.CostEstimate(
            flops=10 * rows * width * SUB, bytes_accessed=14 * rows * width, transcendentals=0
        ),
        name="intra",
    )(*inputs)

    index = lax.axis_index("ctx")
    core = index % 2
    chip = index // 2
    quarter = (chip ^ (chip >> 2)) & 1

    def swap(array, mask):
        return lax.ppermute(array, "ctx", [(i, i ^ mask) for i in range(count_ctx)])

    def mine_and_other(array, which):
        size = array.shape[1] // 2
        low, high = array[:, :size], array[:, size:]
        return jnp.where(which == 0, low, high), jnp.where(which == 0, high, low)

    def in_order(mine, other, which):
        return jnp.concatenate(
            [jnp.where(which == 0, mine, other), jnp.where(which == 0, other, mine)], 1
        )

    def add(a, b):
        return (a.astype(F32) + b.astype(F32)).astype(BF16)

    own_state, other_state = mine_and_other(state, core)
    core_state = swap(other_state, 1)
    chip_sum = add(own_state, core_state)
    own_sum, other_sum = mine_and_other(chip_sum, quarter)
    near_sum = swap(other_sum, 2)
    pair_sum = add(own_sum, near_sum)
    prefix = jnp.zeros(pair_sum.shape[1:], F32)
    suffix = prefix
    for step in (5, 2, 7):
        is_lower = chip < (chip ^ step)
        arrived = swap(jnp.where(is_lower, pair_sum[0], pair_sum[1]), 2 * step).astype(F32)
        prefix = prefix + jnp.where(is_lower, 0.0, arrived)
        suffix = suffix + jnp.where(is_lower, arrived, 0.0)
    is_first = (chip & 1) == 0
    near_wide = near_sum.astype(F32)
    own_wide = own_sum.astype(F32)
    for_near = jnp.stack(
        [
            prefix + jnp.where(is_first, own_wide[0], 0.0),
            suffix + jnp.where(is_first, 0.0, own_wide[1]),
        ]
    ).astype(BF16)
    from_near = swap(for_near, 2)
    mine = jnp.stack(
        [
            prefix + jnp.where(is_first, 0.0, near_wide[0]),
            suffix + jnp.where(is_first, near_wide[1], 0.0),
        ]
    ).astype(BF16)
    outer = in_order(mine, from_near, quarter)
    outer_wide = outer.astype(F32)
    state_wide = own_state.astype(F32)
    core_wide = core_state.astype(F32)
    for_core = jnp.stack(
        [
            outer_wide[0] + jnp.where(core == 0, state_wide[0], 0.0),
            outer_wide[1] + jnp.where(core == 0, 0.0, state_wide[1]),
        ]
    ).astype(BF16)
    from_core = swap(for_core, 1)
    mine = jnp.stack(
        [
            outer_wide[0] + jnp.where(core == 0, 0.0, core_wide[0]),
            outer_wide[1] + jnp.where(core == 0, core_wide[1], 0.0),
        ]
    ).astype(BF16)
    both = in_order(mine, from_core, core)

    return pl.pallas_call(
        final_kernel,
        grid=(pairs,),
        in_specs=[wide_spec] * 6
        + [
            pl.BlockSpec((None, 2, HEAD, HEAD), lambda p: (0, p, 0, 0)),
            pl.BlockSpec((None, 2, HEAD, HEAD), lambda p: (1, p, 0, 0)),
            pl.BlockSpec((2, 2, subs - 1, HEAD, HEAD), lambda p: (0, p, 0, 0, 0)),
        ],
        out_specs=(wide_spec,) * 3,
        out_shape=(wide,) * 3,
        cost_estimate=pl.CostEstimate(
            flops=6 * rows * width * HEAD, bytes_accessed=18 * rows * width, transcendentals=0
        ),
        name="final",
    )(key_vectors, value_vectors, out_grad, *partial, both, both, local)


def solution(mesh):
    spec = P(("dp", "ctx"), "tp")
    return jax.shard_map(
        on_device,
        mesh=mesh,
        in_specs=(spec,) * 4,
        out_specs=(spec,) * 3,
        check_vma=False,
    )
```

time: 204 us -> 53.4 us (0.26); the launches traced: 202 us -> 53.2 us
  matrix products: 87.9 us -> 0 us
  waiting for transfers between devices: 76.6 us -> 12.2 us
  Pallas kernels: 0 us -> 21.9 us
  local copies, waits for them, and re-layouts: 14.9 us -> 0 us
  starting transfers between devices: 0.08 us -> 14.7 us
  between operations: 14.1 us -> 0.75 us
  other arithmetic: 7.85 us -> 3.59 us
    dot_general x58 -> x0, matrix products: 87.9 us -> none  [the longest x8 15.2 us: head_block(): jnp.dot(weights.T, grad_rows, preferred_element_type=jnp.float32)]
    all_gather x2 -> x0, waiting for transfers between devices: 76.6 us -> none  [the longest x1 38.6 us: on_device(): lax.all_gather(local_grad[None], 'ctx', axis=0, tiled=True)]
    pallas_call x0 -> x3, Pallas kernels: none -> 21.9 us  [the longest x1 9.43 us: on_device(): pl.pallas_call(lambda *refs: intra_kernel(factor, *refs), grid=(pairs,),...]
    ppermute x0 -> x7, starting transfers between devices: none -> 14.7 us  [swap(): return lax.ppermute(array, 'ctx', [(i, i ^ mask) for i in range(count_ctx)])]
    ppermute x0 -> x7, waiting for transfers between devices: none -> 12.2 us  [swap(): return lax.ppermute(array, 'ctx', [(i, i ^ mask) for i in range(count_ctx)])]
    unnamed x8 -> x0, local copies, waits for them, and re-layouts: 9.22 us -> none
    reduce_sum x2 -> x0, other arithmetic: 7.84 us -> none  [the longest x1 3.93 us: on_device(): jnp.sum(earlier_mask[:, None, None, None] * pieces[0].astype(jnp.float32)...]
    reshape x3 -> x0, local copies, waits for them, and re-layouts: 5.66 us -> none  [rows_first(): return tensor_in.transpose(1, 0, 2).reshape(count_rows, local_heads * HEAD)]
  transfers between devices with their start and end apart: 2 -> 7, of which waited for: 2 -> 6; matrix products, arithmetic and copies ran while one was open for 6% -> 0% of each run, Pallas kernels for 0% -> 18%
where the time goes in v1:
time: 53.4 us; the launch traced here: 53.2 us
  Pallas kernels  21.9 us (41%)
  starting transfers between devices  14.7 us (28%)
  waiting for transfers between devices  12.2 us (23%)
  other arithmetic  3.59 us (7%)
  between operations  0.75 us (1%)
    ppermute x7, starting transfers between devices, swap(): return lax.ppermute(array, 'ctx', [(i, i ^ mask) for i in range(count_ctx)])  14.7 us
    ppermute x7, waiting for transfers between devices, swap(): return lax.ppermute(array, 'ctx', [(i, i ^ mask) for i in range(count_ctx)])  12.2 us
    pallas_call x1, Pallas kernels, on_device(): pl.pallas_call(lambda *refs: intra_kernel(factor, *refs), grid=(pairs,),...  9.43 us
    pallas_call x1, Pallas kernels, on_device(): pl.pallas_call(final_kernel, grid=(pairs,), in_specs=[wide_spec] * 6 + [p...  7.25 us
    pallas_call x1, Pallas kernels, on_device(): pl.pallas_call(lambda *refs: states_kernel(factor, *refs), grid=(pairs,),...  5.26 us
    convert_element_type x4, other arithmetic, add(): return (a.astype(F32) + b.astype(F32)).astype(BF16)  1.25 us
    select_n x2, other arithmetic, mine_and_other(): return (jnp.where(which == 0, low, high), jnp.where(which == 0, high, low))  1.08 us
  transfers between devices with their start and end apart: 7, of which 6 were waited for; matrix products, arithmetic and copies ran while one was open for 0% of the time, Pallas kernels for 18%

profile of v1, /device:TPU:1, one launch (start us, length us, event | category | flops | bytes accessed | tf_op | source)
XLA Modules:
  0.0 53.2 jit_solution(5795815452708098452)
XLA Ops:
  0.6 5.3 %states.1 = (bf16[2,8,128,128]{3,2,1,0:T(8,128)(2,1)}, bf16[2,8,2,128,128]{4,3,2,1,0:T(8,128)(2,1)}) custom-call(bf16[768,1024]{1,0:T(8,128)(2,1)} %refs_0_.3, bf16[768,1024]{1,0:T(8,128)(2,1)} %k_ref.1, bf16[768,1024]{1,0:T(8,128)(2,1)} %v_ref.1, bf16[768,1024]{1,0:T(8,128)(2,1)} %g_ref.1), custom_call_target="tpu_custom_call" | custom-call | flops 402653184 | bytes 6291456 | tf_op jit(solution)/shard_map/states/pallas_call | solution.py:100
  5.9 1.1 %broadcast_select_fusion.2 = bf16[2,4,128,128]{3,2,1,0:T(8,128)(2,1)S(1)} fusion(pred[]{:T(512)S(6)} %eq.8, bf16[2,8,128,128]{3,2,1,0:T(8,128)(2,1)} %get-tuple-element.11), kind=kLoop, calls=%fused_computation.21 | loop fusion | flops 131072 | bytes 786433 | tf_op jit(solution)/shard_map/jit(_where)/select_n | solution.py:142
  7.0 3.3 %collective-permute-start = (bf16[2,4,128,128]{3,2,1,0:T(8,128)(2,1)S(1)}, bf16[2,4,128,128]{3,2,1,0:T(8,128)(2,1)S(1)}, u32[]{:S(2)}, u32[]{:S(2)}) collective-permute-start(bf16[2,4,128,128]{3,2,1,0:T(8,128)(2,1)S(1)} %broadcast_select_fusion.2), channel_id=1, source_target_pairs={{0,16},{16,0},{32,48},{48,32},{64,80},{80,64},{96,112},{112,96},{1... | collective-permute-start | bytes 786440 | tf_op jit(solution)/shard_map/ppermute | solution.py:137
  10.3 1.2 %collective-permute-done = bf16[2,4,128,128]{3,2,1,0:T(8,128)(2,1)S(1)} collective-permute-done((bf16[2,4,128,128]{3,2,1,0:T(8,128)(2,1)S(1)}, bf16[2,4,128,128]{3,2,1,0:T(8,128)(2,1)S(1)}, u32[]{:S(2)}, u32[]{:S(2)}) %collective-permute-start) | collective-permute-done | bytes 262176 | tf_op jit(solution)/shard_map/ppermute | solution.py:137
  11.4 1.1 %add_convert_fusion = (bf16[2,4,128,128]{3,2,1,0:T(8,128)(2,1)S(1)}, f32[2,4,128,128]{3,2,1,0:T(8,128)S(1)}) fusion(bf16[2,4,128,128]{3,2,1,0:T(8,128)(2,1)S(1)} %collective-permute-done, bf16[2,8,128,128]{3,2,1,0:T(8,128)(2,1)} %get-tuple-element.11, pred[]{:T(512)S(6)} %eq.8), kind=kLoop, calls=%fused_computation.1 | loop fusion | flops 655360 | bytes 1572865 | tf_op jit(solution)/shard_map/convert_element_type | solution.py:150
  12.6 0.1 collective-permute-start.1
  12.7 4.7 %collective-permute-done.1 = bf16[2,2,128,128]{3,2,1,0:T(8,128)(2,1)S(1)} collective-permute-done((bf16[2,2,128,128]{3,2,1,0:T(8,128)(2,1)S(1)}, bf16[2,2,128,128]{3,2,1,0:T(8,128)(2,1)S(1)}, u32[]{:S(2)}, u32[]{:S(2)}) %collective-permute-start.1) | collective-permute-done | bytes 131104 | tf_op jit(solution)/shard_map/ppermute | solution.py:137
  17.4 0.1 add_convert_fusion.1
  17.5 4.8 %collective-permute-start.2 = (bf16[2,128,128]{2,1,0:T(8,128)(2,1)S(1)}, bf16[2,128,128]{2,1,0:T(8,128)(2,1)S(1)}, u32[]{:S(2)}, u32[]{:S(2)}) collective-permute-start(bf16[2,128,128]{2,1,0:T(8,128)(2,1)S(1)} %get-tuple-element.33), channel_id=1, source_target_pairs={{0,160},{16,176},{32,128},{48,144},{64,224},{80,240},{96,192},{112... | collective-permute-start | bytes 196616 | tf_op jit(solution)/shard_map/ppermute | solution.py:137
  22.3 0.0 collective-permute-start.4
  22.3 1.3 %collective-permute-start.3 = (bf16[2,128,128]{2,1,0:T(8,128)(2,1)S(1)}, bf16[2,128,128]{2,1,0:T(8,128)(2,1)S(1)}, u32[]{:S(2)}, u32[]{:S(2)}) collective-permute-start(bf16[2,128,128]{2,1,0:T(8,128)(2,1)S(1)} %get-tuple-element.35), channel_id=1, source_target_pairs={{0,64},{16,80},{32,96},{48,112},{64,0},{80,16},{96,32},{112,48},{1... | collective-permute-start | bytes 196616 | tf_op jit(solution)/shard_map/ppermute | solution.py:137
  23.6 0.3 collective-permute-done.2
  24.0 2.7 %collective-permute-done.4 = bf16[2,128,128]{2,1,0:T(8,128)(2,1)S(1)} collective-permute-done((bf16[2,128,128]{2,1,0:T(8,128)(2,1)S(1)}, bf16[2,128,128]{2,1,0:T(8,128)(2,1)S(1)}, u32[]{:S(2)}, u32[]{:S(2)}) %collective-permute-start.4) | collective-permute-done | bytes 65568 | tf_op jit(solution)/shard_map/ppermute | solution.py:137
  26.6 1.1 %collective-permute-done.3 = bf16[2,128,128]{2,1,0:T(8,128)(2,1)S(1)} collective-permute-done((bf16[2,128,128]{2,1,0:T(8,128)(2,1)S(1)}, bf16[2,128,128]{2,1,0:T(8,128)(2,1)S(1)}, u32[]{:S(2)}, u32[]{:S(2)}) %collective-permute-start.3) | collective-permute-done | bytes 65568 | tf_op jit(solution)/shard_map/ppermute | solution.py:137
  27.7 0.1 fusion.24
  27.8 1.7 %collective-permute-start.5 = (bf16[2,2,128,128]{3,2,1,0:T(8,128)(2,1)S(1)}, bf16[2,2,128,128]{3,2,1,0:T(8,128)(2,1)S(1)}, u32[]{:S(2)}, u32[]{:S(2)}) collective-permute-start(bf16[2,2,128,128]{3,2,1,0:T(8,128)(2,1)S(1)} %pad_maximum_fusion.4), channel_id=1, source_target_pairs={{0,32},{16,48},{32,0},{48,16},{64,96},{80,112},{96,64},{112,80},{1... | collective-permute-start | bytes 393224 | tf_op jit(solution)/shard_map/ppermute | solution.py:137
  29.6 2.3 %collective-permute-done.5 = bf16[2,2,128,128]{3,2,1,0:T(8,128)(2,1)S(1)} collective-permute-done((bf16[2,2,128,128]{3,2,1,0:T(8,128)(2,1)S(1)}, bf16[2,2,128,128]{3,2,1,0:T(8,128)(2,1)S(1)}, u32[]{:S(2)}, u32[]{:S(2)}) %collective-permute-start.5) | collective-permute-done | bytes 131104 | tf_op jit(solution)/shard_map/ppermute | solution.py:137
  31.9 0.1 fusion.7
  32.1 3.5 %collective-permute-start.6 = (bf16[2,4,128,128]{3,2,1,0:T(8,128)(2,1)S(1)}, bf16[2,4,128,128]{3,2,1,0:T(8,128)(2,1)S(1)}, u32[]{:S(2)}, u32[]{:S(2)}) collective-permute-start(bf16[2,4,128,128]{3,2,1,0:T(8,128)(2,1)S(1)} %pad_maximum_fusion.2), channel_id=1, source_target_pairs={{0,16},{16,0},{32,48},{48,32},{64,80},{80,64},{96,112},{112,96},{1... | collective-permute-start | bytes 786440 | tf_op jit(solution)/shard_map/ppermute | solution.py:137
  35.6 9.4 %intra.1 = (bf16[768,1024]{1,0:T(8,128)(2,1)}, bf16[768,1024]{1,0:T(8,128)(2,1)}, bf16[768,1024]{1,0:T(8,128)(2,1)}) custom-call(bf16[768,1024]{1,0:T(8,128)(2,1)} %refs_0_.3, bf16[768,1024]{1,0:T(8,128)(2,1)} %k_ref.1, bf16[768,1024]{1,0:T(8,128)(2,1)} %v_ref.1, bf16[768,1024]{1,0:T(8,128)(2,1)} %g_ref.1), custom_call_target="tpu_custom_call" | custom-call | flops 2013265920 | bytes 11010048 | tf_op jit(solution)/shard_map/intra/pallas_call | solution.py:119
  45.0 0.0 collective-permute-done.6
  45.1 0.9 %pad_maximum_fusion.prefix_ref.suffix_ref = bf16[2,8,128,128]{3,2,1,0:T(8,128)(2,1)} fusion(bf16[2,4,128,128]{3,2,1,0:T(8,128)(2,1)S(1)} %get-tuple-element.22, bf16[2,4,128,128]{3,2,1,0:T(8,128)(2,1)S(1)} %get-tuple-element.21), kind=kLoop, calls=%fused_computation | loop fusion | flops 262144 | bytes 1048576 | tf_op jit(solution)/shard_map/concatenate | solution.py:145
  45.9 7.2 %final.1 = (bf16[768,1024]{1,0:T(8,128)(2,1)}, bf16[768,1024]{1,0:T(8,128)(2,1)}, bf16[768,1024]{1,0:T(8,128)(2,1)}) custom-call(bf16[768,1024]{1,0:T(8,128)(2,1)} %k_ref.1, bf16[768,1024]{1,0:T(8,128)(2,1)} %v_ref.1, bf16[768,1024]{1,0:T(8,128)(2,1)} %g_ref.1, bf16[768,1024]{1,0:T(8,128)(2,1)} %get-tuple-element.8.gq_in, ...), custom_call_target="tpu_custom_call" | custom-call | flops 603979776 | bytes 14155776 | tf_op jit(solution)/shard_map/final/pallas_call | solution.py:200
  (9 shorter events, 0.2 us)
Async XLA Ops:
  7.0 4.5 %collective-permute-start = (bf16[2,4,128,128]{3,2,1,0:T(8,128)(2,1)S(1)}, bf16[2,4,128,128]{3,2,1,0:T(8,128)(2,1)S(1)}, u32[]{:S(2)}, u32[]{:S(2)}) collective-permute-start(bf16[2,4,128,128]{3,2,1,0:T(8,128)(2,1)S(1)} %broadcast_select_fusion.2), channel_id=1, source_target_pairs={{0,16},{16,0},{32,48},{48,32},{64,80},{80,64},{96,112},{112,96},{1... | collective-permute-start | bytes 786440 | tf_op jit(solution)/shard_map/ppermute | solution.py:137
  12.6 4.8 %collective-permute-start.1 = (bf16[2,2,128,128]{3,2,1,0:T(8,128)(2,1)S(1)}, bf16[2,2,128,128]{3,2,1,0:T(8,128)(2,1)S(1)}, u32[]{:S(2)}, u32[]{:S(2)}) collective-permute-start(bf16[2,2,128,128]{3,2,1,0:T(8,128)(2,1)S(1)} %broadcast_select_fusion.5), channel_id=1, source_target_pairs={{0,32},{16,48},{32,0},{48,16},{64,96},{80,112},{96,64},{112,80},{1... | collective-permute-start | bytes 393224 | tf_op jit(solution)/shard_map/ppermute | solution.py:137
  17.5 6.5 %collective-permute-start.2 = (bf16[2,128,128]{2,1,0:T(8,128)(2,1)S(1)}, bf16[2,128,128]{2,1,0:T(8,128)(2,1)S(1)}, u32[]{:S(2)}, u32[]{:S(2)}) collective-permute-start(bf16[2,128,128]{2,1,0:T(8,128)(2,1)S(1)} %get-tuple-element.33), channel_id=1, source_target_pairs={{0,160},{16,176},{32,128},{48,144},{64,224},{80,240},{96,192},{112... | collective-permute-start | bytes 196616 | tf_op jit(solution)/shard_map/ppermute | solution.py:137
  22.3 4.3 %collective-permute-start.4 = (bf16[2,128,128]{2,1,0:T(8,128)(2,1)S(1)}, bf16[2,128,128]{2,1,0:T(8,128)(2,1)S(1)}, u32[]{:S(2)}, u32[]{:S(2)}) collective-permute-start(bf16[2,128,128]{2,1,0:T(8,128)(2,1)S(1)} %get-tuple-element.34), channel_id=1, source_target_pairs={{0,224},{16,240},{32,192},{48,208},{64,160},{80,176},{96,128},{112... | collective-permute-start | bytes 196616 | tf_op jit(solution)/shard_map/ppermute | solution.py:137
  22.3 5.4 %collective-permute-start.3 = (bf16[2,128,128]{2,1,0:T(8,128)(2,1)S(1)}, bf16[2,128,128]{2,1,0:T(8,128)(2,1)S(1)}, u32[]{:S(2)}, u32[]{:S(2)}) collective-permute-start(bf16[2,128,128]{2,1,0:T(8,128)(2,1)S(1)} %get-tuple-element.35), channel_id=1, source_target_pairs={{0,64},{16,80},{32,96},{48,112},{64,0},{80,16},{96,32},{112,48},{1... | collective-permute-start | bytes 196616 | tf_op jit(solution)/shard_map/ppermute | solution.py:137
  27.8 4.0 %collective-permute-start.5 = (bf16[2,2,128,128]{3,2,1,0:T(8,128)(2,1)S(1)}, bf16[2,2,128,128]{3,2,1,0:T(8,128)(2,1)S(1)}, u32[]{:S(2)}, u32[]{:S(2)}) collective-permute-start(bf16[2,2,128,128]{3,2,1,0:T(8,128)(2,1)S(1)} %pad_maximum_fusion.4), channel_id=1, source_target_pairs={{0,32},{16,48},{32,0},{48,16},{64,96},{80,112},{96,64},{112,80},{1... | collective-permute-start | bytes 393224 | tf_op jit(solution)/shard_map/ppermute | solution.py:137
  32.1 12.9 %collective-permute-start.6 = (bf16[2,4,128,128]{3,2,1,0:T(8,128)(2,1)S(1)}, bf16[2,4,128,128]{3,2,1,0:T(8,128)(2,1)S(1)}, u32[]{:S(2)}, u32[]{:S(2)}) collective-permute-start(bf16[2,4,128,128]{3,2,1,0:T(8,128)(2,1)S(1)} %pad_maximum_fusion.2), channel_id=1, source_target_pairs={{0,16},{16,0},{32,48},{48,32},{64,80},{80,64},{96,112},{112,96},{1... | collective-permute-start | bytes 786440 | tf_op jit(solution)/shard_map/ppermute | solution.py:137

commit v2 on v0

v2 whole, which is shorter than its diff:
```python
import math

import jax
import jax.numpy as jnp
from jax import lax
from jax.experimental import pallas as pl
from jax.experimental.pallas import tpu as pltpu
from jax.sharding import PartitionSpec as P

HEAD = 128
SUB = 256
PAIR = 2 * HEAD
F32 = jnp.float32
BF16 = jnp.bfloat16
VMEM = pltpu.VMEM
MIB = 1 << 20

NN = (((1,), (0,)), ((), ()))
NT = (((1,), (1,)), ((), ()))
TN = (((0,), (0,)), ((), ()))


def places():
    index = lax.axis_index("ctx")
    core = lax.rem(index, 2)
    chip = lax.div(index, 2)
    low = lax.rem(chip, 2)
    quarter = lax.rem(low + lax.div(chip, 4), 2)
    return core, chip, low, quarter


def pair_columns(core, quarter, pair):
    of_core = core if pair < 2 else 1 - core
    of_quarter = quarter if pair % 2 == 0 else 1 - quarter
    return pl.ds(pl.multiple_of((2 * of_core + of_quarter) * PAIR, PAIR), PAIR)


def mm(a, b, dims):
    return lax.dot_general(a, b, dims, preferred_element_type=F32)


def call(kernel, name, args, outs, scratch=(), flops=0, traffic=0, limit=16, aliases=None):
    def placed(array, space):
        return array if space is pl.ANY else pltpu.with_memory_space_constraint(array, space)

    out_specs = tuple(
        pl.BlockSpec(memory_space=VMEM if space is VMEM else pltpu.HBM) for space, _ in outs
    )
    out_shape = tuple(
        VMEM(shape, BF16) if space is VMEM else jax.ShapeDtypeStruct(shape, BF16)
        for space, shape in outs
    )
    return pl.pallas_call(
        kernel,
        in_specs=[pl.BlockSpec(memory_space=space) for _, space in args],
        out_specs=out_specs,
        out_shape=out_shape,
        scratch_shapes=list(scratch),
        input_output_aliases=aliases or {},
        compiler_params=pltpu.CompilerParams(vmem_limit_bytes=limit * MIB),
        cost_estimate=pl.CostEstimate(flops=flops, bytes_accessed=traffic, transcendentals=0),
        name=name,
    )(*(placed(array, space) for array, space in args))


def states_kernel(first_pair, factor, *refs):
    sources = refs[:4]
    state_ref, local_ref = refs[-7:-5]
    held = refs[-5:-1]
    sems = refs[-1]
    core, _, _, quarter = places()

    def copy(pair, which):
        return pltpu.make_async_copy(
            sources[which].at[:, pair_columns(core, quarter, first_pair + pair)],
            held[which].at[pair],
            sems.at[pair, which],
        )

    order = (1, 2, 0, 3)
    for pair in range(2):
        for which in order:
            copy(pair, which).start()
    subs = held[0].shape[1] // SUB
    for pair in range(2):
        for kind, (left, right) in enumerate(((1, 2), (0, 3))):
            copy(pair, left).wait()
            copy(pair, right).wait()
            for head in range(2):
                cols = slice(head * HEAD, (head + 1) * HEAD)
                parts = []
                for sub in range(subs):
                    rows = slice(sub * SUB, (sub + 1) * SUB)
                    parts.append(
                        factor * mm(held[left][pair, rows, cols], held[right][pair, rows, cols], TN)
                    )
                if kind == 1:
                    parts = parts[::-1]
                total = parts[0]
                for sub in range(1, subs):
                    local_ref[kind, 2 * pair + head, sub - 1] = total.astype(BF16)
                    total = total + parts[sub]
                state_ref[kind, 2 * pair + head] = total.astype(BF16)


def intra_kernel(factor, q_ref, k_ref, v_ref, g_ref, _, gq_ref, gk_ref, gv_ref):
    row = lax.broadcasted_iota(jnp.int32, (SUB, SUB), 0)
    col = lax.broadcasted_iota(jnp.int32, (SUB, SUB), 1)
    subs = q_ref.shape[1] // SUB
    for pair in range(2):
        for head in range(2):
            cols = slice(head * HEAD, (head + 1) * HEAD)
            for sub in range(subs):
                rows = slice(sub * SUB, (sub + 1) * SUB)
                q, k, v, g = (ref[pair, rows, cols] for ref in (q_ref, k_ref, v_ref, g_ref))
                weights_t = jnp.where(col >= row, factor * mm(k, q, NT), 0.0).astype(BF16)
                upstream = jnp.where(row >= col, factor * mm(g, v, NT), 0.0).astype(BF16)
                gq_ref[pair, rows, cols] = mm(upstream, k, NN).astype(BF16)
                gk_ref[pair, rows, cols] = mm(upstream, q, TN).astype(BF16)
                gv_ref[pair, rows, cols] = mm(weights_t, g, NN).astype(BF16)


def pair_sum_kernel(own_ref, near_ref, _a, _b, _c, for_5, for_2, for_7):
    _, chip, _, _ = places()
    bit0, bit1, bit2 = lax.rem(chip, 2), lax.rem(lax.div(chip, 2), 2), lax.div(chip, 4)
    del bit0
    state = (own_ref[0].astype(F32) + near_ref[0].astype(F32)).astype(BF16)
    grad = (own_ref[1].astype(F32) + near_ref[1].astype(F32)).astype(BF16)
    for_5[...] = jnp.where(bit2 == 0, state, grad)
    for_2[...] = jnp.where(bit1 == 0, state, grad)
    for_7[...] = jnp.where(bit2 == 0, state, grad)


def add_where(base, condition, term):
    return base + jnp.where(condition, term.astype(F32), 0.0)


def pair_scan_kernel(
    from_5, from_2, from_7, own_sum, near_sum, own_state, core_state, _a, _b, _c, outer_ref, near_ref, wide_ref
):
    core, chip, low, _ = places()
    bit1, bit2 = lax.rem(lax.div(chip, 2), 2), lax.div(chip, 4)
    prefix = jnp.zeros(from_5.shape, F32)
    suffix = prefix
    for arrived, bit in ((from_5, bit2), (from_2, bit1), (from_7, bit2)):
        prefix = add_where(prefix, bit == 1, arrived[...])
        suffix = add_where(suffix, bit == 0, arrived[...])
    near_ref[0] = add_where(prefix, low == 0, own_sum[0]).astype(BF16)
    near_ref[1] = add_where(suffix, low == 1, own_sum[1]).astype(BF16)
    prefix = add_where(prefix, low == 1, near_sum[0])
    suffix = add_where(suffix, low == 0, near_sum[1])
    outer_ref[0] = add_where(prefix, core == 0, own_state[0, 0:2]).astype(BF16)
    outer_ref[1] = add_where(suffix, core == 1, own_state[1, 0:2]).astype(BF16)
    wide_ref[0] = add_where(prefix, core == 1, core_state[0, 0:2]).astype(BF16)
    wide_ref[1] = add_where(suffix, core == 0, core_state[1, 0:2]).astype(BF16)


def near_scan_kernel(from_near, outer, own_state, core_state, _, for_core_ref, wide_ref):
    core, _, _, _ = places()
    prefix = from_near[0].astype(F32)
    suffix = from_near[1].astype(F32)
    for_core_ref[:, 0:2] = outer[...]
    for_core_ref[0, 2:4] = add_where(prefix, core == 0, own_state[0, 2:4]).astype(BF16)
    for_core_ref[1, 2:4] = add_where(suffix, core == 1, own_state[1, 2:4]).astype(BF16)
    wide_ref[0] = add_where(prefix, core == 1, core_state[0, 2:4]).astype(BF16)
    wide_ref[1] = add_where(suffix, core == 0, core_state[1, 2:4]).astype(BF16)


def block_diagonal(first, second):
    zero = jnp.zeros_like(first)
    return jnp.concatenate(
        [jnp.concatenate([first, zero], 1), jnp.concatenate([zero, second], 1)], 0
    )


def final_kernel(first_pair, count, *refs):
    k_ref, v_ref, g_ref, gq_in, gk_in, gv_in, wide_ref, local_ref = refs[:8]
    outs = refs[-8:-5]
    token = refs[-5]
    buffers = refs[-4:-1]
    sems = refs[-1]
    core, _, _, quarter = places()
    subs = k_ref.shape[1] // SUB
    token[...] = jnp.zeros(token.shape, token.dtype)
    copies = []
    for step in range(count):
        pair = first_pair % 2 + step

        def of_sub(kind, terms):
            heads = []
            for head in range(2):
                wide = wide_ref[kind, 2 * step + head]
                if terms > 0:
                    wide = (
                        wide.astype(F32) + local_ref[kind, 2 * pair + head, terms - 1].astype(F32)
                    ).astype(BF16)
                heads.append(wide)
            return block_diagonal(*heads)

        for sub in range(subs):
            rows = slice(sub * SUB, (sub + 1) * SUB)
            prefix = of_sub(0, sub)
            suffix = of_sub(1, subs - 1 - sub)
            for buffer, base, rows_in, weight, dims in (
                (buffers[0], gq_in, g_ref, prefix, NT),
                (buffers[1], gk_in, v_ref, suffix, NT),
                (buffers[2], gv_in, k_ref, suffix, NN),
            ):
                buffer[step, rows, :] = (
                    base[pair, rows, :].astype(F32) + mm(rows_in[pair, rows, :], weight, dims)
                ).astype(BF16)
        for which in range(3):
            copy = pltpu.make_async_copy(
                buffers[which].at[step],
                outs[which].at[:, pair_columns(core, quarter, first_pair + step)],
                sems.at[step, which],
            )
            copy.start()
            copies.append(copy)
    for copy in copies:
        copy.wait()


def on_device(*inputs):
    rows, width = inputs[0].shape
    count_ctx = lax.axis_size("ctx")
    factor = 1.0 / math.sqrt(HEAD * rows * count_ctx)
    subs = rows // SUB
    held = (2, rows, PAIR)
    square = (HEAD, HEAD)

    def swap(array, mask):
        return lax.ppermute(array, "ctx", [(i, i ^ mask) for i in range(count_ctx)])

    def states(first_pair, name, *after):
        out = call(
            lambda *refs: states_kernel(first_pair, factor, *refs),
            name,
            [(array, pltpu.HBM) for array in inputs] + [(array, pl.ANY) for array in after],
            [(VMEM, (2, 4) + square), (VMEM, (2, 4, subs - 1) + square)] + [(VMEM, held)] * 4,
            scratch=[pltpu.SemaphoreType.DMA((2, 4))],
            flops=2 * rows * width * HEAD,
            traffic=4 * rows * width,
        )
        return out[0], out[1], out[2:]

    def intra(arrays, name, after):
        return call(
            lambda *refs: intra_kernel(factor, *refs),
            name,
            [(array, VMEM) for array in arrays] + [(after, pl.ANY)],
            [(VMEM, held)] * 3,
            flops=5 * rows * width * SUB,
            traffic=7 * rows * width,
        )

    def final(first_pair, count, name, arrays, partial, wide, local, outs):
        before = [(array, pltpu.HBM) for array in outs]
        return call(
            lambda *refs: final_kernel(first_pair, count, *refs),
            name,
            [(array, VMEM) for array in (*arrays[1:], *partial, wide, local)] + before,
            [(pltpu.HBM, (rows, width))] * 3 + [(VMEM, (16, HEAD))],
            scratch=[pltpu.VMEM((count, rows, PAIR), BF16)] * 3 + [pltpu.SemaphoreType.DMA((count, 3))],
            flops=3 * rows * PAIR * PAIR * count,
            traffic=6 * rows * PAIR * count,
            aliases={8 + i: i for i in range(len(before))},
        )

    other_state, other_local, other_held = states(2, "states_other")
    core_state = swap(other_state, 1)
    own_state, own_local, own_held = states(0, "states_own", other_state)
    chip_sum = (own_state.astype(F32) + core_state.astype(F32)).astype(BF16)
    own_sum, other_sum = chip_sum[:, 0:2], chip_sum[:, 2:4]
    near_sum = swap(other_sum, 2)
    other_partial = intra(other_held, "intra_other", other_sum)

    sends = call(
        pair_sum_kernel,
        "pair_sum",
        [(own_sum, VMEM), (near_sum, VMEM)] + [(array, pl.ANY) for array in other_partial],
        [(VMEM, (2,) + square)] * 3,
    )
    arrived = [swap(array, 2 * mask) for array, mask in zip(sends, (5, 2, 7))]
    own_partial = intra(own_held, "intra_own", sends[0])
    outer, for_near, wide_0 = call(
        pair_scan_kernel,
        "pair_scan",
        [(array, VMEM) for array in (*arrived, own_sum, near_sum, own_state, core_state)]
        + [(array, pl.ANY) for array in own_partial],
        [(VMEM, (2, 2) + square)] * 3,
    )
    from_near = swap(for_near, 2)
    *outs, token = final(0, 1, "final_0", own_held, own_partial, wide_0, own_local, ())
    for_core, wide_1 = call(
        near_scan_kernel,
        "near_scan",
        [(array, VMEM) for array in (from_near, outer, own_state, core_state)] + [(token, pl.ANY)],
        [(VMEM, (2, 4) + square), (VMEM, (2, 2) + square)],
    )
    from_core = swap(for_core, 1)
    *outs, token = final(1, 1, "final_1", own_held, own_partial, wide_1, own_local, outs)
    *outs, token = final(2, 2, "final_2", other_held, other_partial, from_core, other_local, outs)
    return tuple(outs)


def solution(mesh):
    spec = P(("dp", "ctx"), "tp")
    return jax.shard_map(
        on_device,
        mesh=mesh,
        in_specs=(spec,) * 4,
        out_specs=(spec,) * 3,
        check_vma=False,
    )
```

time: 204 us -> 38.4 us (0.19); the launches traced: 202 us -> 38.3 us
  matrix products: 87.9 us -> 0 us
  waiting for transfers between devices: 76.6 us -> 4.99 us
  Pallas kernels: 0 us -> 18 us
  local copies, waits for them, and re-layouts: 14.9 us -> 0.02 us
  starting transfers between devices: 0.08 us -> 14.4 us
  between operations: 14.1 us -> 0.9 us
  other arithmetic: 7.85 us -> 0.07 us
    dot_general x58 -> x0, matrix products: 87.9 us -> none  [the longest x8 15.2 us: head_block(): jnp.dot(weights.T, grad_rows, preferred_element_type=jnp.float32)]
    all_gather x2 -> x0, waiting for transfers between devices: 76.6 us -> none  [the longest x1 38.6 us: on_device(): lax.all_gather(local_grad[None], 'ctx', axis=0, tiled=True)]
    pallas_call x0 -> x10, Pallas kernels: none -> 18 us  [call(): pl.pallas_call(kernel, in_specs=[pl.BlockSpec(memory_space=space) for _,...]
    ppermute x0 -> x7, starting transfers between devices: none -> 14.4 us  [swap(): return lax.ppermute(array, 'ctx', [(i, i ^ mask) for i in range(count_ctx)])]
    unnamed x8 -> x0, local copies, waits for them, and re-layouts: 9.22 us -> none
    reduce_sum x2 -> x0, other arithmetic: 7.84 us -> none  [the longest x1 3.93 us: on_device(): jnp.sum(earlier_mask[:, None, None, None] * pieces[0].astype(jnp.float32)...]
    reshape x3 -> x0, local copies, waits for them, and re-layouts: 5.66 us -> none  [rows_first(): return tensor_in.transpose(1, 0, 2).reshape(count_rows, local_heads * HEAD)]
    ppermute x0 -> x7, waiting for transfers between devices: none -> 4.99 us  [swap(): return lax.ppermute(array, 'ctx', [(i, i ^ mask) for i in range(count_ctx)])]
  transfers between devices with their start and end apart: 2 -> 7, of which waited for: 2 -> 3; matrix products, arithmetic and copies ran while one was open for 6% -> 0% of each run, Pallas kernels for 0% -> 33%
where the time goes in v2:
time: 38.4 us; the launch traced here: 38.3 us
  Pallas kernels  18 us (47%)
  starting transfers between devices  14.4 us (38%)
  waiting for transfers between devices  4.99 us (13%)
  between operations  0.9 us (2%)
    pallas_call x10, Pallas kernels, call(): pl.pallas_call(kernel, in_specs=[pl.BlockSpec(memory_space=space) for _,...  18 us
    ppermute x7, starting transfers between devices, swap(): return lax.ppermute(array, 'ctx', [(i, i ^ mask) for i in range(count_ctx)])  14.4 us
    ppermute x7, waiting for transfers between devices, swap(): return lax.ppermute(array, 'ctx', [(i, i ^ mask) for i in range(count_ctx)])  4.99 us
  transfers between devices with their start and end apart: 7, of which 3 were waited for; matrix products, arithmetic and copies ran while one was open for 0% of the time, Pallas kernels for 33%

profile of v2, /device:TPU:1, one launch (start us, length us, event | category | flops | bytes accessed | tf_op | source)
XLA Modules:
  0.0 38.3 jit_solution(3859682375868220583)
XLA Ops:
  0.6 2.5 %states_other.1 = (bf16[2,4,128,128]{3,2,1,0:T(8,128)(2,1)S(1)}, bf16[2,4,2,128,128]{4,3,2,1,0:T(8,128)(2,1)S(1)}, bf16[2,768,256]{2,1,0:T(8,128)(2,1)S(1)}, bf1...) custom-call(bf16[768,1024]{1,0:T(8,128)(2,1)} %refs_0_.3, ...), custom_call_target="tpu_custom_call" | custom-call | flops 201326592 | bytes 3145728 | tf_op jit(solution)/shard_map/states_other/pallas_call | solution.py:53
  3.1 3.3 %collective-permute-start = (bf16[2,4,128,128]{3,2,1,0:T(8,128)(2,1)S(1)}, bf16[2,4,128,128]{3,2,1,0:T(8,128)(2,1)S(1)}, u32[]{:S(2)}, u32[]{:S(2)}) collective-permute-start(bf16[2,4,128,128]{3,2,1,0:T(8,128)(2,1)S(1)} %get-tuple-element.43.refs_4_), channel_id=1, source_target_pairs={{0,16},{16,0},{32,48},{48,32},{64,80},{80,64},{96,112},{112,96},{1... | collective-permute-start | bytes 786440 | tf_op jit(solution)/shard_map/ppermute | solution.py:233
  6.4 2.4 %states_own.1 = (bf16[2,4,128,128]{3,2,1,0:T(8,128)(2,1)S(1)}, bf16[2,4,2,128,128]{4,3,2,1,0:T(8,128)(2,1)S(1)}, bf16[2,768,256]{2,1,0:T(8,128)(2,1)S(1)}, bf16[...) custom-call(bf16[768,1024]{1,0:T(8,128)(2,1)} %refs_0_.3, ...), custom_call_target="tpu_custom_call" | custom-call | flops 201326592 | bytes 3145728 | tf_op jit(solution)/shard_map/states_own/pallas_call | solution.py:53
  8.9 0.0 collective-permute-done.core_state
  8.9 0.1 add_convert_fusion
  9.0 0.1 collective-permute-start.1
  9.1 3.3 %intra_other.1 = (bf16[2,768,256]{2,1,0:T(8,128)(2,1)S(1)}, bf16[2,768,256]{2,1,0:T(8,128)(2,1)S(1)}, bf16[2,768,256]{2,1,0:T(8,128)(2,1)S(1)}) custom-call(bf16[2,768,256]{2,1,0:T(8,128)(2,1)S(1)} %get-tuple-element.42.refs_0_, bf16[2,768,256]{2,1,0:T(8,128)(2,1)S(1)} %get-tuple-element.39.refs_1_.refs_0_, ...), custom_call_target="tpu_custom_call" | custom-call | flops 1006632960 | bytes 5505024 | tf_op jit(solution)/shard_map/intra_other/pallas_call | solution.py:53
  12.4 1.8 %collective-permute-done.1.near_ref.near_sum = bf16[2,2,128,128]{3,2,1,0:T(8,128)(2,1)S(1)} collective-permute-done((bf16[2,2,128,128]{3,2,1,0:T(8,128)(2,1)S(1)}, bf16[2,2,128,128]{3,2,1,0:T(8,128)(2,1)S(1)}, u32[]{:S(2)}, u32[]{:S(2)}) %collective-permute-start.1) | collective-permute-done | bytes 131104 | tf_op jit(solution)/shard_map/ppermute | solution.py:233
  14.2 4.8 %collective-permute-start.2 = (bf16[2,128,128]{2,1,0:T(8,128)(2,1)S(1)}, bf16[2,128,128]{2,1,0:T(8,128)(2,1)S(1)}, u32[]{:S(2)}, u32[]{:S(2)}) collective-permute-start(bf16[2,128,128]{2,1,0:T(8,128)(2,1)S(1)} %get-tuple-element.48.refs_4_), channel_id=1, source_target_pairs={{0,160},{16,176},{32,128},{48,144},{64,224},{80,240},{96,192},{112... | collective-permute-start | bytes 196616 | tf_op jit(solution)/shard_map/ppermute | solution.py:233
  19.0 1.2 %collective-permute-start.3 = (bf16[2,128,128]{2,1,0:T(8,128)(2,1)S(1)}, bf16[2,128,128]{2,1,0:T(8,128)(2,1)S(1)}, u32[]{:S(2)}, u32[]{:S(2)}) collective-permute-start(bf16[2,128,128]{2,1,0:T(8,128)(2,1)S(1)} %get-tuple-element.49), channel_id=1, source_target_pairs={{0,64},{16,80},{32,96},{48,112},{64,0},{80,16},{96,32},{112,48},{1... | collective-permute-start | bytes 196616 | tf_op jit(solution)/shard_map/ppermute | solution.py:233
  20.2 0.0 collective-permute-start.4
  20.2 3.3 %intra_own.1 = (bf16[2,768,256]{2,1,0:T(8,128)(2,1)S(1)}, bf16[2,768,256]{2,1,0:T(8,128)(2,1)S(1)}, bf16[2,768,256]{2,1,0:T(8,128)(2,1)S(1)}) custom-call(bf16[2,768,256]{2,1,0:T(8,128)(2,1)S(1)} %get-tuple-element.51.refs_0_, bf16[2,768,256]{2,1,0:T(8,128)(2,1)S(1)} %get-tuple-element.52.refs_1_.refs_0_, ...), custom_call_target="tpu_custom_call" | custom-call | flops 1006632960 | bytes 5505024 | tf_op jit(solution)/shard_map/intra_own/pallas_call | solution.py:53
  23.5 0.0 collective-permute-done.2.from_5
  23.5 2.2 %collective-permute-done.3.from_2 = bf16[2,128,128]{2,1,0:T(8,128)(2,1)S(1)} collective-permute-done((bf16[2,128,128]{2,1,0:T(8,128)(2,1)S(1)}, bf16[2,128,128]{2,1,0:T(8,128)(2,1)S(1)}, u32[]{:S(2)}, u32[]{:S(2)}) %collective-permute-start.3) | collective-permute-done | bytes 65568 | tf_op jit(solution)/shard_map/ppermute | solution.py:233
  25.8 0.0 collective-permute-done.4.from_7
  25.8 0.2 pair_scan.1
  26.0 1.6 %collective-permute-start.5 = (bf16[2,2,128,128]{3,2,1,0:T(8,128)(2,1)S(1)}, bf16[2,2,128,128]{3,2,1,0:T(8,128)(2,1)S(1)}, u32[]{:S(2)}, u32[]{:S(2)}) collective-permute-start(bf16[2,2,128,128]{3,2,1,0:T(8,128)(2,1)S(1)} %get-tuple-element.58), channel_id=1, source_target_pairs={{0,32},{16,48},{32,0},{48,16},{64,96},{80,112},{96,64},{112,80},{1... | collective-permute-start | bytes 393224 | tf_op jit(solution)/shard_map/ppermute | solution.py:233
  27.6 1.5 %final_0.1 = (bf16[768,1024]{1,0:T(8,128)(2,1)}, bf16[768,1024]{1,0:T(8,128)(2,1)}, bf16[768,1024]{1,0:T(8,128)(2,1)}, bf16[16,128]{1,0:T(8,128)(2,1)S(1)}) custom-call(bf16[2,768,256]{2,1,0:T(8,128)(2,1)S(1)} %get-tuple-element.52.refs_1_.refs_0_, bf16[2,768,256]{2,1,0:T(8,128)(2,1)S(1)} %get-tuple-element.53.refs_2_.refs_1_, ...), custom_call_target="tpu_custom_call" | custom-call | flops 150994944 | bytes 1179648 | tf_op jit(solution)/shard_map/final_0/pallas_call | solution.py:53
  29.1 1.0 %collective-permute-done.5.from_near = bf16[2,2,128,128]{3,2,1,0:T(8,128)(2,1)S(1)} collective-permute-done((bf16[2,2,128,128]{3,2,1,0:T(8,128)(2,1)S(1)}, bf16[2,2,128,128]{3,2,1,0:T(8,128)(2,1)S(1)}, u32[]{:S(2)}, u32[]{:S(2)}) %collective-permute-start.5) | collective-permute-done | bytes 131104 | tf_op jit(solution)/shard_map/ppermute | solution.py:233
  30.1 0.1 near_scan.1
  30.2 3.3 %collective-permute-start.6 = (bf16[2,4,128,128]{3,2,1,0:T(8,128)(2,1)S(1)}, bf16[2,4,128,128]{3,2,1,0:T(8,128)(2,1)S(1)}, u32[]{:S(2)}, u32[]{:S(2)}) collective-permute-start(bf16[2,4,128,128]{3,2,1,0:T(8,128)(2,1)S(1)} %get-tuple-element.63), channel_id=1, source_target_pairs={{0,16},{16,0},{32,48},{48,32},{64,80},{80,64},{96,112},{112,96},{1... | collective-permute-start | bytes 786440 | tf_op jit(solution)/shard_map/ppermute | solution.py:233
  33.5 2.1 %final_1.1 = (bf16[768,1024]{1,0:T(8,128)(2,1)}, bf16[768,1024]{1,0:T(8,128)(2,1)}, bf16[768,1024]{1,0:T(8,128)(2,1)}, bf16[16,128]{1,0:T(8,128)(2,1)}) custom-call(bf16[2,768,256]{2,1,0:T(8,128)(2,1)S(1)} %get-tuple-element.52.refs_1_.refs_0_, ...), custom_call_target="tpu_custom_call", output_to_operand_aliasing={{0}: (8, {}), {1}: (9, {}), {2}: (10, {})} | custom-call | flops 150994944 | bytes 1179648 | tf_op jit(solution)/shard_map/final_1/pallas_call | solution.py:53
  35.6 0.0 collective-permute-done.6.refs_6_
  35.6 2.5 %final_2.1 = (bf16[768,1024]{1,0:T(8,128)(2,1)}, bf16[768,1024]{1,0:T(8,128)(2,1)}, bf16[768,1024]{1,0:T(8,128)(2,1)}, bf16[16,128]{1,0:T(8,128)(2,1)}) custom-call(bf16[2,768,256]{2,1,0:T(8,128)(2,1)S(1)} %get-tuple-element.39.refs_1_.refs_0_, ...), custom_call_target="tpu_custom_call", output_to_operand_aliasing={{0}: (8, {}), {1}: (9, {}), {2}: (10, {})} | custom-call | flops 301989888 | bytes 2359296 | tf_op jit(solution)/shard_map/final_2/pallas_call | solution.py:53
  (2 shorter events, 0.1 us)
Async XLA Ops:
  3.1 5.8 %collective-permute-start = (bf16[2,4,128,128]{3,2,1,0:T(8,128)(2,1)S(1)}, bf16[2,4,128,128]{3,2,1,0:T(8,128)(2,1)S(1)}, u32[]{:S(2)}, u32[]{:S(2)}) collective-permute-start(bf16[2,4,128,128]{3,2,1,0:T(8,128)(2,1)S(1)} %get-tuple-element.43.refs_4_), channel_id=1, source_target_pairs={{0,16},{16,0},{32,48},{48,32},{64,80},{80,64},{96,112},{112,96},{1... | collective-permute-start | bytes 786440 | tf_op jit(solution)/shard_map/ppermute | solution.py:233
  9.0 5.2 %collective-permute-start.1 = (bf16[2,2,128,128]{3,2,1,0:T(8,128)(2,1)S(1)}, bf16[2,2,128,128]{3,2,1,0:T(8,128)(2,1)S(1)}, u32[]{:S(2)}, u32[]{:S(2)}) collective-permute-start(bf16[2,2,128,128]{3,2,1,0:T(8,128)(2,1)S(1)} %get-tuple-element.76.refs_4_), channel_id=1, source_target_pairs={{0,32},{16,48},{32,0},{48,16},{64,96},{80,112},{96,64},{112,80},{1... | collective-permute-start | bytes 393224 | tf_op jit(solution)/shard_map/ppermute | solution.py:233
  14.2 9.3 %collective-permute-start.2 = (bf16[2,128,128]{2,1,0:T(8,128)(2,1)S(1)}, bf16[2,128,128]{2,1,0:T(8,128)(2,1)S(1)}, u32[]{:S(2)}, u32[]{:S(2)}) collective-permute-start(bf16[2,128,128]{2,1,0:T(8,128)(2,1)S(1)} %get-tuple-element.48.refs_4_), channel_id=1, source_target_pairs={{0,160},{16,176},{32,128},{48,144},{64,224},{80,240},{96,192},{112... | collective-permute-start | bytes 196616 | tf_op jit(solution)/shard_map/ppermute | solution.py:233
  19.0 6.7 %collective-permute-start.3 = (bf16[2,128,128]{2,1,0:T(8,128)(2,1)S(1)}, bf16[2,128,128]{2,1,0:T(8,128)(2,1)S(1)}, u32[]{:S(2)}, u32[]{:S(2)}) collective-permute-start(bf16[2,128,128]{2,1,0:T(8,128)(2,1)S(1)} %get-tuple-element.49), channel_id=1, source_target_pairs={{0,64},{16,80},{32,96},{48,112},{64,0},{80,16},{96,32},{112,48},{1... | collective-permute-start | bytes 196616 | tf_op jit(solution)/shard_map/ppermute | solution.py:233
  20.2 5.5 %collective-permute-start.4 = (bf16[2,128,128]{2,1,0:T(8,128)(2,1)S(1)}, bf16[2,128,128]{2,1,0:T(8,128)(2,1)S(1)}, u32[]{:S(2)}, u32[]{:S(2)}) collective-permute-start(bf16[2,128,128]{2,1,0:T(8,128)(2,1)S(1)} %get-tuple-element.50), channel_id=1, source_target_pairs={{0,224},{16,240},{32,192},{48,208},{64,160},{80,176},{96,128},{112... | collective-permute-start | bytes 196616 | tf_op jit(solution)/shard_map/ppermute | solution.py:233
  26.0 4.1 %collective-permute-start.5 = (bf16[2,2,128,128]{3,2,1,0:T(8,128)(2,1)S(1)}, bf16[2,2,128,128]{3,2,1,0:T(8,128)(2,1)S(1)}, u32[]{:S(2)}, u32[]{:S(2)}) collective-permute-start(bf16[2,2,128,128]{3,2,1,0:T(8,128)(2,1)S(1)} %get-tuple-element.58), channel_id=1, source_target_pairs={{0,32},{16,48},{32,0},{48,16},{64,96},{80,112},{96,64},{112,80},{1... | collective-permute-start | bytes 393224 | tf_op jit(solution)/shard_map/ppermute | solution.py:233
  30.2 5.5 %collective-permute-start.6 = (bf16[2,4,128,128]{3,2,1,0:T(8,128)(2,1)S(1)}, bf16[2,4,128,128]{3,2,1,0:T(8,128)(2,1)S(1)}, u32[]{:S(2)}, u32[]{:S(2)}) collective-permute-start(bf16[2,4,128,128]{3,2,1,0:T(8,128)(2,1)S(1)} %get-tuple-element.63), channel_id=1, source_target_pairs={{0,16},{16,0},{32,48},{48,32},{64,80},{80,64},{96,112},{112,96},{1... | collective-permute-start | bytes 786440 | tf_op jit(solution)/shard_map/ppermute | solution.py:233

commit v3 on v2

v3 whole, which is shorter than its diff:
```python
import math

import jax
import jax.numpy as jnp
from jax import lax
from jax.experimental import pallas as pl
from jax.experimental.pallas import tpu as pltpu
from jax.sharding import PartitionSpec as P

HEAD = 128
SUB = 256
PAIR = 2 * HEAD
F32 = jnp.float32
BF16 = jnp.bfloat16
VMEM = pltpu.VMEM
MIB = 1 << 20
STEPS = (2, 5, 7)

NN = (((1,), (0,)), ((), ()))
NT = (((1,), (1,)), ((), ()))
TN = (((0,), (0,)), ((), ()))


def places():
    index = lax.axis_index("ctx")
    core = lax.rem(index, 2)
    chip = lax.div(index, 2)
    low = lax.rem(chip, 2)
    quarter = lax.rem(low + lax.div(chip, 4), 2)
    return core, chip, low, quarter


def pair_columns(core, quarter, pair):
    of_core = core if pair < 2 else 1 - core
    of_quarter = quarter if pair % 2 == 0 else 1 - quarter
    return pl.ds(pl.multiple_of((2 * of_core + of_quarter) * PAIR, PAIR), PAIR)


def mm(a, b, dims):
    return lax.dot_general(a, b, dims, preferred_element_type=F32)


def call(kernel, name, args, outs, scratch=(), limit=16, aliases=None):
    def placed(array, space):
        return array if space is pl.ANY else pltpu.with_memory_space_constraint(array, space)

    out_specs = tuple(
        pl.BlockSpec(memory_space=VMEM if space is VMEM else pltpu.HBM) for space, _ in outs
    )
    out_shape = tuple(
        VMEM(shape, BF16) if space is VMEM else jax.ShapeDtypeStruct(shape, BF16)
        for space, shape in outs
    )
    return pl.pallas_call(
        kernel,
        in_specs=[pl.BlockSpec(memory_space=space) for _, space in args],
        out_specs=out_specs,
        out_shape=out_shape,
        scratch_shapes=list(scratch),
        input_output_aliases=aliases or {},
        compiler_params=pltpu.CompilerParams(vmem_limit_bytes=limit * MIB),
        cost_estimate=pl.CostEstimate(flops=0, bytes_accessed=0, transcendentals=0),
        name=name,
    )(*(placed(array, space) for array, space in args))


def states_kernel(pairs, factor, *refs):
    sources = refs[:4]
    results = refs[-5 * len(pairs) - 2 : -1]
    state_ref = results[0]
    sems = refs[-1]
    core, _, _, quarter = places()
    subs = sources[0].shape[0] // SUB

    def copy(step, which):
        return pltpu.make_async_copy(
            sources[which].at[:, pair_columns(core, quarter, pairs[step])],
            results[5 * step + 2 + which],
            sems.at[step, which],
        )

    for step in range(len(pairs)):
        for which in (1, 2, 0, 3):
            copy(step, which).start()
    for step in range(len(pairs)):
        local_ref, *held = results[5 * step + 1 : 5 * step + 6]
        for kind, (left, right) in enumerate(((1, 2), (0, 3))):
            copy(step, left).wait()
            copy(step, right).wait()
            for head in range(2):
                cols = slice(head * HEAD, (head + 1) * HEAD)
                parts = []
                for sub in range(subs):
                    rows = slice(sub * SUB, (sub + 1) * SUB)
                    parts.append(factor * mm(held[left][rows, cols], held[right][rows, cols], TN))
                if kind == 1:
                    parts = parts[::-1]
                total = parts[0]
                for sub in range(1, subs):
                    local_ref[kind, head, sub - 1] = total.astype(BF16)
                    total = total + parts[sub]
                state_ref[step, kind, head] = total.astype(BF16)


def intra_kernel(factor, q_ref, k_ref, v_ref, g_ref, _, gq_ref, gk_ref, gv_ref):
    row = lax.broadcasted_iota(jnp.int32, (SUB, SUB), 0)
    col = lax.broadcasted_iota(jnp.int32, (SUB, SUB), 1)
    subs = q_ref.shape[0] // SUB
    for head in range(2):
        cols = slice(head * HEAD, (head + 1) * HEAD)
        for sub in range(subs):
            rows = slice(sub * SUB, (sub + 1) * SUB)
            q, k, v, g = (ref[rows, cols] for ref in (q_ref, k_ref, v_ref, g_ref))
            weights_t = jnp.where(col >= row, factor * mm(k, q, NT), 0.0).astype(BF16)
            upstream = jnp.where(row >= col, factor * mm(g, v, NT), 0.0).astype(BF16)
            gq_ref[rows, cols] = mm(upstream, k, NN).astype(BF16)
            gk_ref[rows, cols] = mm(upstream, q, TN).astype(BF16)
            gv_ref[rows, cols] = mm(weights_t, g, NN).astype(BF16)


def add_where(base, condition, term):
    return base + jnp.where(condition, term.astype(F32), 0.0)


def upper_bit(chip, step):
    return lax.rem(lax.div(chip, 1 << (step.bit_length() - 1)), 2)


def pair_sum_kernel(own_ref, core_ref, near_sum, *refs):
    own_state, core_state = own_ref.at[0], core_ref.at[1]
    outs = refs[-3:]
    _, chip, _, _ = places()
    state, grad = (
        (own_state[i].astype(F32) + core_state[i].astype(F32) + near_sum[i].astype(F32)).astype(BF16)
        for i in range(2)
    )
    for step, out in zip(STEPS, outs):
        out[...] = jnp.where(upper_bit(chip, step) == 0, state, grad)


def pair_scan_kernel(*refs):
    arrived = refs[:3]
    own_ref, core_ref, near_sum = refs[3:6]
    own_state, core_state = own_ref.at[0], core_ref.at[1]
    near_ref, outer_ref, wide_ref = refs[-3:]
    core, chip, low, _ = places()
    sums = [jnp.zeros(arrived[0].shape, F32)] * 2
    for step, term in zip(STEPS, arrived):
        bit = upper_bit(chip, step)
        sums = [add_where(sums[i], bit == 1 - i, term[...]) for i in range(2)]
    for i in range(2):
        own = own_state[i].astype(F32)
        other = core_state[i].astype(F32)
        near_ref[i] = add_where(sums[i], low == i, own + other).astype(BF16)
        total = add_where(sums[i], low == 1 - i, near_sum[i])
        outer_ref[i] = add_where(total, core == i, own).astype(BF16)
        wide_ref[i] = add_where(total, core == 1 - i, other).astype(BF16)


def near_scan_kernel(from_near, own_ref, core_ref, *refs):
    own_state, core_state = own_ref.at[0], core_ref.at[0]
    outer_ref, wide_ref = refs[-2:]
    core, _, _, _ = places()
    for i in range(2):
        total = from_near[i].astype(F32)
        outer_ref[i] = add_where(total, core == i, own_state[i]).astype(BF16)
        wide_ref[i] = add_where(total, core == 1 - i, core_state[i]).astype(BF16)


def block_diagonal(first, second):
    zero = jnp.zeros_like(first)
    return jnp.concatenate(
        [jnp.concatenate([first, zero], 1), jnp.concatenate([zero, second], 1)], 0
    )


def final_kernel(pairs, ready, keep, *refs):
    waiting = refs[8 * len(pairs) : 8 * len(pairs) + 3 * len(ready)]
    sems = refs[-1]
    core, _, _, quarter = places()
    copies = []
    count = 3 * len(pairs)
    if keep:
        *outs, token = refs[-2 - count - 3 * bool(ready) : -1 - count]
    else:
        *outs, token = refs[-2 - count - 3 : -1 - count]
    buffers = refs[-1 - count : -1]
    token[...] = jnp.zeros(token.shape, token.dtype)

    def send(buffer, pair, which, row, size):
        rows = pl.ds(row, size)
        copy = pltpu.make_async_copy(
            buffer.at[rows],
            outs[which].at[rows, pair_columns(core, quarter, pair)],
            sems.at[len(copies)],
        )
        copy.start()
        copies.append(copy)

    for step, pair in enumerate(ready):
        for which in range(3):
            buffer = waiting[3 * step + which]
            send(buffer, pair, which, 0, buffer.shape[0])
    for step, pair in enumerate(pairs):
        k_ref, v_ref, g_ref, gq_in, gk_in, gv_in, wide_ref, local_ref = refs[8 * step : 8 * step + 8]
        subs = k_ref.shape[0] // SUB

        def of_sub(kind, terms):
            heads = []
            for head in range(2):
                wide = wide_ref[kind, head]
                if terms > 0:
                    wide = (
                        wide.astype(F32) + local_ref[kind, head, terms - 1].astype(F32)
                    ).astype(BF16)
                heads.append(wide)
            return block_diagonal(*heads)

        for sub in range(subs):
            rows = slice(sub * SUB, (sub + 1) * SUB)
            prefix = of_sub(0, sub)
            suffix = of_sub(1, subs - 1 - sub)
            for which, (base, rows_in, weight, dims) in enumerate(
                ((gq_in, g_ref, prefix, NT), (gk_in, v_ref, suffix, NT), (gv_in, k_ref, suffix, NN))
            ):
                buffer = buffers[3 * step + which]
                buffer[rows, :] = (
                    base[rows, :].astype(F32) + mm(rows_in[rows, :], weight, dims)
                ).astype(BF16)
                if not keep:
                    send(buffer, pair, which, sub * SUB, SUB)
    for copy in copies:
        copy.wait()


def on_device(*inputs):
    rows, width = inputs[0].shape
    count_ctx = lax.axis_size("ctx")
    factor = 1.0 / math.sqrt(HEAD * rows * count_ctx)
    subs = rows // SUB
    held = (rows, PAIR)
    square = (HEAD, HEAD)

    def swap(array, mask):
        return lax.ppermute(array, "ctx", [(i, i ^ mask) for i in range(count_ctx)])

    def states(pairs, *after):
        state, *out = call(
            lambda *refs: states_kernel(pairs, factor, *refs),
            "states_" + "_".join(map(str, pairs)),
            [(array, pltpu.HBM) for array in inputs] + [(array, pl.ANY) for array in after],
            [(VMEM, (len(pairs), 2, 2) + square)]
            + ([(VMEM, (2, 2, subs - 1) + square)] + [(VMEM, held)] * 4) * len(pairs),
            scratch=[pltpu.SemaphoreType.DMA((len(pairs), 4))],
        )
        return state, *((out[i], out[i + 1 : i + 5]) for i in range(0, len(out), 5))

    def intra(pair, arrays, after):
        return call(
            lambda *refs: intra_kernel(factor, *refs),
            f"intra_{pair}",
            [(array, VMEM) for array in arrays] + [(after, pl.ANY)],
            [(VMEM, held)] * 3,
        )

    def scan(kernel, name, args, after, count):
        return call(
            kernel,
            name,
            [(array, VMEM) for array in args] + [(array, pl.ANY) for array in after],
            count,
        )

    def final(parts, outs, ready=None, keep=False):
        ready = ready or {}
        args = []
        for arrays, partial, wide, local in parts.values():
            args += [(array, VMEM) for array in (*arrays[1:], *partial, wide, local)]
        for arrays in ready.values():
            args += [(array, VMEM) for array in arrays]
        count = len(parts)
        sends = 3 * len(ready) + (0 if keep else 3 * subs * count)
        to_outs = [(pltpu.HBM, (rows, width))] * (3 if sends else 0)
        results = [(VMEM, held)] * 3 * count
        out = call(
            lambda *refs: final_kernel(tuple(parts), tuple(ready), keep, *refs),
            "final_" + "_".join(map(str, parts)),
            args + [(array, pltpu.HBM) for array in outs],
            to_outs + [(VMEM, (16, HEAD))] + (results if keep else []),
            scratch=([] if keep else [pltpu.VMEM(held, BF16)] * 3 * count)
            + [pltpu.SemaphoreType.DMA((max(sends, 1),))],
            aliases={len(args) + i: i for i in range(len(outs))},
        )
        return out[: len(to_outs)], out[len(to_outs)], out[len(to_outs) + 1 :]

    quarter = (2, 2) + square
    state_32, (local_3, held_3), (local_2, held_2) = states((3, 2))
    core_10 = swap(state_32, 1)
    state_1, (local_1, held_1) = states((1,), state_32)
    sum_1 = (state_1[0].astype(F32) + core_10[0].astype(F32)).astype(BF16)
    near_0 = swap(sum_1, 2)
    state_0, (local_0, held_0) = states((0,), sum_1)
    partial_3 = intra(3, held_3, sum_1)
    sends = scan(
        pair_sum_kernel, "pair_sum", (state_0, core_10, near_0), partial_3, [(VMEM, (2,) + square)] * 3
    )
    arrived = [swap(array, 2 * step) for step, array in zip(STEPS, sends)]
    partial_1 = intra(1, held_1, sends[0])
    partial_0 = intra(0, held_0, sends[0])
    for_near, outer_0, wide_0 = scan(
        pair_scan_kernel,
        "pair_scan",
        (*arrived, state_0, core_10, near_0),
        (*partial_1, *partial_0),
        [(VMEM, quarter)] * 3,
    )
    from_near = swap(for_near, 2)
    wide_2 = swap(outer_0, 1)
    partial_2 = intra(2, held_2, for_near)
    outs, token, _ = final(
        {0: (held_0, partial_0, wide_0, local_0), 2: (held_2, partial_2, wide_2, local_2)}, ()
    )
    outer_1, wide_1 = scan(
        near_scan_kernel,
        "near_scan",
        (from_near, state_1, core_10),
        (token,),
        [(VMEM, quarter)] * 2,
    )
    wide_3 = swap(outer_1, 1)
    _, _, ready_1 = final({1: (held_1, partial_1, wide_1, local_1)}, (), keep=True)
    outs, _, _ = final({3: (held_3, partial_3, wide_3, local_3)}, outs, ready={1: ready_1})
    return tuple(outs)


def solution(mesh):
    spec = P(("dp", "ctx"), "tp")
    return jax.shard_map(
        on_device,
        mesh=mesh,
        in_specs=(spec,) * 4,
        out_specs=(spec,) * 3,
        check_vma=False,
    )
```

time: 38.4 us -> 35.9 us (0.935)
  waiting for transfers between devices: 4.99 us -> 2.99 us
  starting transfers between devices: 14.4 us -> 13.6 us
    ppermute x7 -> x8, waiting for transfers between devices: 4.99 us -> 2.99 us  [swap(): return lax.ppermute(array, 'ctx', [(i, i ^ mask) for i in range(count_ctx)])]
    ppermute x7 -> x8, starting transfers between devices: 14.4 us -> 13.6 us  [swap(): return lax.ppermute(array, 'ctx', [(i, i ^ mask) for i in range(count_ctx)])]
    pallas_call x10 -> x13, Pallas kernels: 18 us -> 18.2 us  [call(): pl.pallas_call(kernel, in_specs=[pl.BlockSpec(memory_space=space) for _,...]
  transfers between devices with their start and end apart: 7 -> 8, of which waited for: 3 -> 3; matrix products, arithmetic and copies ran while one was open for 0% -> 0% of each run, Pallas kernels for 33% -> 37%
where the time goes in v3:
time: 35.9 us; the launch traced here: 35.7 us
  Pallas kernels  18.2 us (51%)
  starting transfers between devices  13.6 us (38%)
  waiting for transfers between devices  2.99 us (8%)
  between operations  0.92 us (3%)
    pallas_call x13, Pallas kernels, call(): pl.pallas_call(kernel, in_specs=[pl.BlockSpec(memory_space=space) for _,...  18.2 us
    ppermute x8, starting transfers between devices, swap(): return lax.ppermute(array, 'ctx', [(i, i ^ mask) for i in range(count_ctx)])  13.6 us
    ppermute x8, waiting for transfers between devices, swap(): return lax.ppermute(array, 'ctx', [(i, i ^ mask) for i in range(count_ctx)])  2.99 us
  transfers between devices with their start and end apart: 8, of which 3 were waited for; matrix products, arithmetic and copies ran while one was open for 0% of the time, Pallas kernels for 37%

profile of v3, /device:TPU:1, one launch (start us, length us, event | category | flops | bytes accessed | tf_op | source)
XLA Modules:
  0.0 35.7 jit_solution(6251286876915391169)
XLA Ops:
  0.6 2.5 %states_3_2.1 = (bf16[2,2,2,128,128]{4,3,2,1,0:T(8,128)(2,1)S(1)}, bf16[2,2,2,128,128]{4,3,2,1,0:T(8,128)(2,1)S(1)}, bf16[768,256]{1,0:T(8,128)(2,1)S(1)}, bf16[...) custom-call(bf16[768,1024]{1,0:T(8,128)(2,1)} %refs_0_.5, ...), custom_call_target="tpu_custom_call" | custom-call | tf_op jit(solution)/shard_map/states_3_2/pallas_call | solution.py:54
  3.1 3.3 %collective-permute-start = (bf16[2,2,2,128,128]{4,3,2,1,0:T(8,128)(2,1)S(1)}, bf16[2,2,2,128,128]{4,3,2,1,0:T(8,128)(2,1)S(1)}, u32[]{:S(2)}, u32[]{:S(2)}) collective-permute-start(bf16[2,2,2,128,128]{4,3,2,1,0:T(8,128)(2,1)S(1)} %get-tuple-element.60.refs_4_), channel_id=1, source_target_pairs={{0,16},{16,0},{32,48},{48,32},{64,80},{80,64},{96,112},{112,96},{1... | collective-permute-start | bytes 786440 | tf_op jit(solution)/shard_map/ppermute | solution.py:245
  6.4 1.8 %states_1.1 = (bf16[1,2,2,128,128]{4,3,2,1,0:T(8,128)(2,1)S(1)}, bf16[2,2,2,128,128]{4,3,2,1,0:T(8,128)(2,1)S(1)}, bf16[768,256]{1,0:T(8,128)(2,1)S(1)}, bf16[76...) custom-call(bf16[768,1024]{1,0:T(8,128)(2,1)} %refs_0_.5, ...), custom_call_target="tpu_custom_call" | custom-call | tf_op jit(solution)/shard_map/states_1/pallas_call | solution.py:54
  8.3 0.1 collective-permute-start.1
  8.4 1.8 %states_0.1 = (bf16[1,2,2,128,128]{4,3,2,1,0:T(8,128)(2,1)S(1)}, bf16[2,2,2,128,128]{4,3,2,1,0:T(8,128)(2,1)S(1)}, bf16[768,256]{1,0:T(8,128)(2,1)S(1)}, bf16[76...) custom-call(bf16[768,1024]{1,0:T(8,128)(2,1)} %refs_0_.5, ...), custom_call_target="tpu_custom_call" | custom-call | tf_op jit(solution)/shard_map/states_0/pallas_call | solution.py:54
  10.2 1.8 %intra_3.1 = (bf16[768,256]{1,0:T(8,128)(2,1)S(1)}, bf16[768,256]{1,0:T(8,128)(2,1)S(1)}, bf16[768,256]{1,0:T(8,128)(2,1)S(1)}) custom-call(bf16[768,256]{1,0:T(8,128)(2,1)S(1)} %get-tuple-element.59.refs_0_, bf16[768,256]{1,0:T(8,128)(2,1)S(1)} %get-tuple-element.56.refs_1_.refs_0_, bf16[768,256]{1,0:T(8,128)(2,1)S(1)} %get-tuple-element.57.refs_2_.refs_1_, ...), custom_call_target="tpu_custom_call" | custom-call | tf_op jit(solution)/shard_map/intra_3/pallas_call | solution.py:54
  12.0 1.5 %collective-permute-done.1.near_sum.refs_5_ = bf16[2,2,128,128]{3,2,1,0:T(8,128)(2,1)S(1)} collective-permute-done((bf16[2,2,128,128]{3,2,1,0:T(8,128)(2,1)S(1)}, bf16[2,2,128,128]{3,2,1,0:T(8,128)(2,1)S(1)}, u32[]{:S(2)}, u32[]{:S(2)}) %collective-permute-start.1) | collective-permute-done | bytes 131104 | tf_op jit(solution)/shard_map/ppermute | solution.py:245
  13.5 0.1 pair_sum.1
  13.5 4.8 %collective-permute-start.3 = (bf16[2,128,128]{2,1,0:T(8,128)(2,1)S(1)}, bf16[2,128,128]{2,1,0:T(8,128)(2,1)S(1)}, u32[]{:S(2)}, u32[]{:S(2)}) collective-permute-start(bf16[2,128,128]{2,1,0:T(8,128)(2,1)S(1)} %get-tuple-element.67), channel_id=1, source_target_pairs={{0,160},{16,176},{32,128},{48,144},{64,224},{80,240},{96,192},{112... | collective-permute-start | bytes 196616 | tf_op jit(solution)/shard_map/ppermute | solution.py:245
  18.4 1.3 %collective-permute-start.2 = (bf16[2,128,128]{2,1,0:T(8,128)(2,1)S(1)}, bf16[2,128,128]{2,1,0:T(8,128)(2,1)S(1)}, u32[]{:S(2)}, u32[]{:S(2)}) collective-permute-start(bf16[2,128,128]{2,1,0:T(8,128)(2,1)S(1)} %get-tuple-element.66.refs_4_), channel_id=1, source_target_pairs={{0,64},{16,80},{32,96},{48,112},{64,0},{80,16},{96,32},{112,48},{1... | collective-permute-start | bytes 196616 | tf_op jit(solution)/shard_map/ppermute | solution.py:245
  19.6 1.7 %intra_0.1 = (bf16[768,256]{1,0:T(8,128)(2,1)S(1)}, bf16[768,256]{1,0:T(8,128)(2,1)S(1)}, bf16[768,256]{1,0:T(8,128)(2,1)S(1)}) custom-call(bf16[768,256]{1,0:T(8,128)(2,1)S(1)} %get-tuple-element.76.refs_0_, bf16[768,256]{1,0:T(8,128)(2,1)S(1)} %get-tuple-element.77.refs_1_.refs_0_, bf16[768,256]{1,0:T(8,128)(2,1)S(1)} %get-tuple-element.78.refs_2_.refs_1_, ...), custom_call_target="tpu_custom_call" | custom-call | tf_op jit(solution)/shard_map/intra_0/pallas_call | solution.py:54
  21.4 1.8 %intra_1.1 = (bf16[768,256]{1,0:T(8,128)(2,1)S(1)}, bf16[768,256]{1,0:T(8,128)(2,1)S(1)}, bf16[768,256]{1,0:T(8,128)(2,1)S(1)}) custom-call(bf16[768,256]{1,0:T(8,128)(2,1)S(1)} %get-tuple-element.69.refs_0_, bf16[768,256]{1,0:T(8,128)(2,1)S(1)} %get-tuple-element.70.refs_1_.refs_0_, bf16[768,256]{1,0:T(8,128)(2,1)S(1)} %get-tuple-element.71.refs_2_.refs_1_, ...), custom_call_target="tpu_custom_call" | custom-call | tf_op jit(solution)/shard_map/intra_1/pallas_call | solution.py:54
  23.2 1.2 %collective-permute-done.2.refs_0_ = bf16[2,128,128]{2,1,0:T(8,128)(2,1)S(1)} collective-permute-done((bf16[2,128,128]{2,1,0:T(8,128)(2,1)S(1)}, bf16[2,128,128]{2,1,0:T(8,128)(2,1)S(1)}, u32[]{:S(2)}, u32[]{:S(2)}) %collective-permute-start.2) | collective-permute-done | bytes 65568 | tf_op jit(solution)/shard_map/ppermute | solution.py:245
  24.4 0.2 pair_scan.1
  24.6 1.1 %collective-permute-start.6 = (bf16[2,2,128,128]{3,2,1,0:T(8,128)(2,1)S(1)}, bf16[2,2,128,128]{3,2,1,0:T(8,128)(2,1)S(1)}, u32[]{:S(2)}, u32[]{:S(2)}) collective-permute-start(bf16[2,2,128,128]{3,2,1,0:T(8,128)(2,1)S(1)} %get-tuple-element.93), channel_id=1, source_target_pairs={{0,16},{16,0},{32,48},{48,32},{64,80},{80,64},{96,112},{112,96},{1... | collective-permute-start | bytes 393224 | tf_op jit(solution)/shard_map/ppermute | solution.py:245
  25.8 2.0 %collective-permute-start.5 = (bf16[2,2,128,128]{3,2,1,0:T(8,128)(2,1)S(1)}, bf16[2,2,128,128]{3,2,1,0:T(8,128)(2,1)S(1)}, u32[]{:S(2)}, u32[]{:S(2)}) collective-permute-start(bf16[2,2,128,128]{3,2,1,0:T(8,128)(2,1)S(1)} %get-tuple-element.83.refs_4_), channel_id=1, source_target_pairs={{0,32},{16,48},{32,0},{48,16},{64,96},{80,112},{96,64},{112,80},{1... | collective-permute-start | bytes 393224 | tf_op jit(solution)/shard_map/ppermute | solution.py:245
  27.8 1.7 %intra_2.1 = (bf16[768,256]{1,0:T(8,128)(2,1)S(1)}, bf16[768,256]{1,0:T(8,128)(2,1)S(1)}, bf16[768,256]{1,0:T(8,128)(2,1)S(1)}) custom-call(bf16[768,256]{1,0:T(8,128)(2,1)S(1)} %get-tuple-element.89.refs_0_, bf16[768,256]{1,0:T(8,128)(2,1)S(1)} %get-tuple-element.86.refs_1_.refs_8_, bf16[768,256]{1,0:T(8,128)(2,1)S(1)} %get-tuple-element.87.refs_2_.refs_9_, ...), custom_call_target="tpu_custom_call" | custom-call | tf_op jit(solution)/shard_map/intra_2/pallas_call | solution.py:54
  29.5 1.9 %final_0_2.1 = (bf16[768,1024]{1,0:T(8,128)(2,1)}, bf16[768,1024]{1,0:T(8,128)(2,1)}, bf16[768,1024]{1,0:T(8,128)(2,1)}, bf16[16,128]{1,0:T(8,128)(2,1)S(1)}) custom-call(bf16[768,256]{1,0:T(8,128)(2,1)S(1)} %get-tuple-element.77.refs_1_.refs_0_, bf16[768,256]{1,0:T(8,128)(2,1)S(1)} %get-tuple-element.78.refs_2_.refs_1_, ...), custom_call_target="tpu_custom_call" | custom-call | tf_op jit(solution)/shard_map/final_0_2/pallas_call | solution.py:54
  31.4 0.0 collective-permute-done.5.from_near
  31.4 0.1 near_scan.1
  31.5 0.9 %collective-permute-start.7 = (bf16[2,2,128,128]{3,2,1,0:T(8,128)(2,1)S(1)}, bf16[2,2,128,128]{3,2,1,0:T(8,128)(2,1)S(1)}, u32[]{:S(2)}, u32[]{:S(2)}) collective-permute-start(bf16[2,2,128,128]{3,2,1,0:T(8,128)(2,1)S(1)} %get-tuple-element.96), channel_id=1, source_target_pairs={{0,16},{16,0},{32,48},{48,32},{64,80},{80,64},{96,112},{112,96},{1... | collective-permute-start | bytes 393224 | tf_op jit(solution)/shard_map/ppermute | solution.py:245
  32.4 0.7 %final_1.1 = (bf16[16,128]{1,0:T(8,128)(2,1)}, bf16[768,256]{1,0:T(8,128)(2,1)S(1)}, bf16[768,256]{1,0:T(8,128)(2,1)S(1)}, bf16[768,256]{1,0:T(8,128)(2,1)S(1)}) custom-call(bf16[768,256]{1,0:T(8,128)(2,1)S(1)} %get-tuple-element.70.refs_1_.refs_0_, bf16[768,256]{1,0:T(8,128)(2,1)S(1)} %get-tuple-element.71.refs_2_.refs_1_, ...), custom_call_target="tpu_custom_call" | custom-call | tf_op jit(solution)/shard_map/final_1/pallas_call | solution.py:54
  33.1 0.3 collective-permute-done.7.refs_6_
  33.4 2.2 %final_3.1 = (bf16[768,1024]{1,0:T(8,128)(2,1)}, bf16[768,1024]{1,0:T(8,128)(2,1)}, bf16[768,1024]{1,0:T(8,128)(2,1)}, bf16[16,128]{1,0:T(8,128)(2,1)}) custom-call(bf16[768,256]{1,0:T(8,128)(2,1)S(1)} %get-tuple-element.56.refs_1_.refs_0_, ...), custom_call_target="tpu_custom_call", output_to_operand_aliasing={{0}: (11, {}), {1}: (12, {}), {2}: (13, {})} | custom-call | tf_op jit(solution)/shard_map/final_3/pallas_call | solution.py:54
  (6 shorter events, 0.1 us)
Async XLA Ops:
  3.1 5.1 %collective-permute-start = (bf16[2,2,2,128,128]{4,3,2,1,0:T(8,128)(2,1)S(1)}, bf16[2,2,2,128,128]{4,3,2,1,0:T(8,128)(2,1)S(1)}, u32[]{:S(2)}, u32[]{:S(2)}) collective-permute-start(bf16[2,2,2,128,128]{4,3,2,1,0:T(8,128)(2,1)S(1)} %get-tuple-element.60.refs_4_), channel_id=1, source_target_pairs={{0,16},{16,0},{32,48},{48,32},{64,80},{80,64},{96,112},{112,96},{1... | collective-permute-start | bytes 786440 | tf_op jit(solution)/shard_map/ppermute | solution.py:245
  8.3 5.2 %collective-permute-start.1 = (bf16[2,2,128,128]{3,2,1,0:T(8,128)(2,1)S(1)}, bf16[2,2,128,128]{3,2,1,0:T(8,128)(2,1)S(1)}, u32[]{:S(2)}, u32[]{:S(2)}) collective-permute-start(bf16[2,2,128,128]{3,2,1,0:T(8,128)(2,1)S(1)} %fusion.refs_4_), channel_id=1, source_target_pairs={{0,32},{16,48},{32,0},{48,16},{64,96},{80,112},{96,64},{112,80},{1... | collective-permute-start | bytes 393224 | tf_op jit(solution)/shard_map/ppermute | solution.py:245
  13.5 9.6 %collective-permute-start.3 = (bf16[2,128,128]{2,1,0:T(8,128)(2,1)S(1)}, bf16[2,128,128]{2,1,0:T(8,128)(2,1)S(1)}, u32[]{:S(2)}, u32[]{:S(2)}) collective-permute-start(bf16[2,128,128]{2,1,0:T(8,128)(2,1)S(1)} %get-tuple-element.67), channel_id=1, source_target_pairs={{0,160},{16,176},{32,128},{48,144},{64,224},{80,240},{96,192},{112... | collective-permute-start | bytes 196616 | tf_op jit(solution)/shard_map/ppermute | solution.py:245
  18.4 4.8 %collective-permute-start.4 = (bf16[2,128,128]{2,1,0:T(8,128)(2,1)S(1)}, bf16[2,128,128]{2,1,0:T(8,128)(2,1)S(1)}, u32[]{:S(2)}, u32[]{:S(2)}) collective-permute-start(bf16[2,128,128]{2,1,0:T(8,128)(2,1)S(1)} %get-tuple-element.68), channel_id=1, source_target_pairs={{0,224},{16,240},{32,192},{48,208},{64,160},{80,176},{96,128},{112... | collective-permute-start | bytes 196616 | tf_op jit(solution)/shard_map/ppermute | solution.py:245
  18.4 6.0 %collective-permute-start.2 = (bf16[2,128,128]{2,1,0:T(8,128)(2,1)S(1)}, bf16[2,128,128]{2,1,0:T(8,128)(2,1)S(1)}, u32[]{:S(2)}, u32[]{:S(2)}) collective-permute-start(bf16[2,128,128]{2,1,0:T(8,128)(2,1)S(1)} %get-tuple-element.66.refs_4_), channel_id=1, source_target_pairs={{0,64},{16,80},{32,96},{48,112},{64,0},{80,16},{96,32},{112,48},{1... | collective-permute-start | bytes 196616 | tf_op jit(solution)/shard_map/ppermute | solution.py:245
  24.6 4.9 %collective-permute-start.6 = (bf16[2,2,128,128]{3,2,1,0:T(8,128)(2,1)S(1)}, bf16[2,2,128,128]{3,2,1,0:T(8,128)(2,1)S(1)}, u32[]{:S(2)}, u32[]{:S(2)}) collective-permute-start(bf16[2,2,128,128]{3,2,1,0:T(8,128)(2,1)S(1)} %get-tuple-element.93), channel_id=1, source_target_pairs={{0,16},{16,0},{32,48},{48,32},{64,80},{80,64},{96,112},{112,96},{1... | collective-permute-start | bytes 393224 | tf_op jit(solution)/shard_map/ppermute | solution.py:245
  25.8 5.7 %collective-permute-start.5 = (bf16[2,2,128,128]{3,2,1,0:T(8,128)(2,1)S(1)}, bf16[2,2,128,128]{3,2,1,0:T(8,128)(2,1)S(1)}, u32[]{:S(2)}, u32[]{:S(2)}) collective-permute-start(bf16[2,2,128,128]{3,2,1,0:T(8,128)(2,1)S(1)} %get-tuple-element.83.refs_4_), channel_id=1, source_target_pairs={{0,32},{16,48},{32,0},{48,16},{64,96},{80,112},{96,64},{112,80},{1... | collective-permute-start | bytes 393224 | tf_op jit(solution)/shard_map/ppermute | solution.py:245
  31.5 1.9 %collective-permute-start.7 = (bf16[2,2,128,128]{3,2,1,0:T(8,128)(2,1)S(1)}, bf16[2,2,128,128]{3,2,1,0:T(8,128)(2,1)S(1)}, u32[]{:S(2)}, u32[]{:S(2)}) collective-permute-start(bf16[2,2,128,128]{3,2,1,0:T(8,128)(2,1)S(1)} %get-tuple-element.96), channel_id=1, source_target_pairs={{0,16},{16,0},{32,48},{48,32},{64,80},{80,64},{96,112},{112,96},{1... | collective-permute-start | bytes 393224 | tf_op jit(solution)/shard_map/ppermute | solution.py:245

commit v4 on v3

--- a/solution.py
+++ b/solution.py
@@ -14,7 +14,7 @@
 BF16 = jnp.bfloat16
 VMEM = pltpu.VMEM
 MIB = 1 << 20
-STEPS = (2, 5, 7)
+STEPS = (5,7,2)
 
 NN = (((1,), (0,)), ((), ()))
 NT = (((1,), (1,)), ((), ()))
@@ -317,19 +317,23 @@
     from_near = swap(for_near, 2)
     wide_2 = swap(outer_0, 1)
     partial_2 = intra(2, held_2, for_near)
-    outs, token, _ = final(
-        {0: (held_0, partial_0, wide_0, local_0), 2: (held_2, partial_2, wide_2, local_2)}, ()
-    )
+    outs, token, _ = final({0: (held_0, partial_0, wide_0, local_0)}, ())
     outer_1, wide_1 = scan(
         near_scan_kernel,
         "near_scan",
         (from_near, state_1, core_10),
-        (token,),
+        (token, *partial_2),
         [(VMEM, quarter)] * 2,
     )
     wide_3 = swap(outer_1, 1)
-    _, _, ready_1 = final({1: (held_1, partial_1, wide_1, local_1)}, (), keep=True)
-    outs, _, _ = final({3: (held_3, partial_3, wide_3, local_3)}, outs, ready={1: ready_1})
+    _, _, kept = final(
+        {1: (held_1, partial_1, wide_1, local_1), 2: (held_2, partial_2, wide_2, local_2)},
+        (),
+        keep=True,
+    )
+    outs, _, _ = final(
+        {3: (held_3, partial_3, wide_3, local_3)}, outs, ready={1: kept[:3], 2: kept[3:]}
+    )
     return tuple(outs)
 
 

time: 35.9 us -> 35.7 us (level)
  Pallas kernels: 18.2 us -> 18.7 us
  starting transfers between devices: 13.6 us -> 13.1 us
    pallas_call x13, Pallas kernels: 18.2 us -> 18.7 us  [call(): pl.pallas_call(kernel, in_specs=[pl.BlockSpec(memory_space=space) for _,...]
    ppermute x8, starting transfers between devices: 13.6 us -> 13.1 us  [swap(): return lax.ppermute(array, 'ctx', [(i, i ^ mask) for i in range(count_ctx)])]
  transfers between devices with their start and end apart: 8 -> 8, of which waited for: 3 -> 2; matrix products, arithmetic and copies ran while one was open for 0% -> 0% of each run, Pallas kernels for 37% -> 38%
where the time goes in v4:
time: 35.7 us; the launch traced here: 35.5 us
  Pallas kernels  18.7 us (52%)
  starting transfers between devices  13.1 us (37%)
  waiting for transfers between devices  2.74 us (8%)
  between operations  0.94 us (3%)
    pallas_call x13, Pallas kernels, call(): pl.pallas_call(kernel, in_specs=[pl.BlockSpec(memory_space=space) for _,...  18.7 us
    ppermute x8, starting transfers between devices, swap(): return lax.ppermute(array, 'ctx', [(i, i ^ mask) for i in range(count_ctx)])  13.1 us
    ppermute x8, waiting for transfers between devices, swap(): return lax.ppermute(array, 'ctx', [(i, i ^ mask) for i in range(count_ctx)])  2.74 us
  transfers between devices with their start and end apart: 8, of which 2 were waited for; matrix products, arithmetic and copies ran while one was open for 0% of the time, Pallas kernels for 38%

profile of v4, /device:TPU:1, one launch (start us, length us, event | category | flops | bytes accessed | tf_op | source)
XLA Modules:
  0.0 35.5 jit_solution(13340492744473711628)
XLA Ops:
  0.6 2.5 %states_3_2.1 = (bf16[2,2,2,128,128]{4,3,2,1,0:T(8,128)(2,1)S(1)}, bf16[2,2,2,128,128]{4,3,2,1,0:T(8,128)(2,1)S(1)}, bf16[768,256]{1,0:T(8,128)(2,1)S(1)}, bf16[...) custom-call(bf16[768,1024]{1,0:T(8,128)(2,1)} %refs_0_.5, ...), custom_call_target="tpu_custom_call" | custom-call | tf_op jit(solution)/shard_map/states_3_2/pallas_call | solution.py:54
  3.1 3.3 %collective-permute-start = (bf16[2,2,2,128,128]{4,3,2,1,0:T(8,128)(2,1)S(1)}, bf16[2,2,2,128,128]{4,3,2,1,0:T(8,128)(2,1)S(1)}, u32[]{:S(2)}, u32[]{:S(2)}) collective-permute-start(bf16[2,2,2,128,128]{4,3,2,1,0:T(8,128)(2,1)S(1)} %get-tuple-element.63.refs_4_), channel_id=1, source_target_pairs={{0,16},{16,0},{32,48},{48,32},{64,80},{80,64},{96,112},{112,96},{1... | collective-permute-start | bytes 786440 | tf_op jit(solution)/shard_map/ppermute | solution.py:245
  6.4 1.8 %states_1.1 = (bf16[1,2,2,128,128]{4,3,2,1,0:T(8,128)(2,1)S(1)}, bf16[2,2,2,128,128]{4,3,2,1,0:T(8,128)(2,1)S(1)}, bf16[768,256]{1,0:T(8,128)(2,1)S(1)}, bf16[76...) custom-call(bf16[768,1024]{1,0:T(8,128)(2,1)} %refs_0_.5, ...), custom_call_target="tpu_custom_call" | custom-call | tf_op jit(solution)/shard_map/states_1/pallas_call | solution.py:54
  8.3 0.1 collective-permute-start.1
  8.4 1.8 %states_0.1 = (bf16[1,2,2,128,128]{4,3,2,1,0:T(8,128)(2,1)S(1)}, bf16[2,2,2,128,128]{4,3,2,1,0:T(8,128)(2,1)S(1)}, bf16[768,256]{1,0:T(8,128)(2,1)S(1)}, bf16[76...) custom-call(bf16[768,1024]{1,0:T(8,128)(2,1)} %refs_0_.5, ...), custom_call_target="tpu_custom_call" | custom-call | tf_op jit(solution)/shard_map/states_0/pallas_call | solution.py:54
  10.2 1.8 %intra_3.1 = (bf16[768,256]{1,0:T(8,128)(2,1)S(1)}, bf16[768,256]{1,0:T(8,128)(2,1)S(1)}, bf16[768,256]{1,0:T(8,128)(2,1)S(1)}) custom-call(bf16[768,256]{1,0:T(8,128)(2,1)S(1)} %get-tuple-element.62.refs_0_, bf16[768,256]{1,0:T(8,128)(2,1)S(1)} %get-tuple-element.59.refs_1_.refs_0_, bf16[768,256]{1,0:T(8,128)(2,1)S(1)} %get-tuple-element.60.refs_2_.refs_1_, ...), custom_call_target="tpu_custom_call" | custom-call | tf_op jit(solution)/shard_map/intra_3/pallas_call | solution.py:54
  12.0 1.5 %collective-permute-done.1.near_sum.refs_5_ = bf16[2,2,128,128]{3,2,1,0:T(8,128)(2,1)S(1)} collective-permute-done((bf16[2,2,128,128]{3,2,1,0:T(8,128)(2,1)S(1)}, bf16[2,2,128,128]{3,2,1,0:T(8,128)(2,1)S(1)}, u32[]{:S(2)}, u32[]{:S(2)}) %collective-permute-start.1) | collective-permute-done | bytes 131104 | tf_op jit(solution)/shard_map/ppermute | solution.py:245
  13.5 0.1 pair_sum.1
  13.5 4.8 %collective-permute-start.2 = (bf16[2,128,128]{2,1,0:T(8,128)(2,1)S(1)}, bf16[2,128,128]{2,1,0:T(8,128)(2,1)S(1)}, u32[]{:S(2)}, u32[]{:S(2)}) collective-permute-start(bf16[2,128,128]{2,1,0:T(8,128)(2,1)S(1)} %get-tuple-element.69.refs_4_), channel_id=1, source_target_pairs={{0,160},{16,176},{32,128},{48,144},{64,224},{80,240},{96,192},{112... | collective-permute-start | bytes 196616 | tf_op jit(solution)/shard_map/ppermute | solution.py:245
  18.4 0.0 collective-permute-start.3
  18.4 1.3 %collective-permute-start.4 = (bf16[2,128,128]{2,1,0:T(8,128)(2,1)S(1)}, bf16[2,128,128]{2,1,0:T(8,128)(2,1)S(1)}, u32[]{:S(2)}, u32[]{:S(2)}) collective-permute-start(bf16[2,128,128]{2,1,0:T(8,128)(2,1)S(1)} %get-tuple-element.71), channel_id=1, source_target_pairs={{0,64},{16,80},{32,96},{48,112},{64,0},{80,16},{96,32},{112,48},{1... | collective-permute-start | bytes 196616 | tf_op jit(solution)/shard_map/ppermute | solution.py:245
  19.6 1.7 %intra_1.1 = (bf16[768,256]{1,0:T(8,128)(2,1)S(1)}, bf16[768,256]{1,0:T(8,128)(2,1)S(1)}, bf16[768,256]{1,0:T(8,128)(2,1)S(1)}) custom-call(bf16[768,256]{1,0:T(8,128)(2,1)S(1)} %get-tuple-element.72.refs_0_, bf16[768,256]{1,0:T(8,128)(2,1)S(1)} %get-tuple-element.73.refs_1_.refs_0_, bf16[768,256]{1,0:T(8,128)(2,1)S(1)} %get-tuple-element.74.refs_2_.refs_1_, ...), custom_call_target="tpu_custom_call" | custom-call | tf_op jit(solution)/shard_map/intra_1/pallas_call | solution.py:54
  21.4 1.7 %intra_0.1 = (bf16[768,256]{1,0:T(8,128)(2,1)S(1)}, bf16[768,256]{1,0:T(8,128)(2,1)S(1)}, bf16[768,256]{1,0:T(8,128)(2,1)S(1)}) custom-call(bf16[768,256]{1,0:T(8,128)(2,1)S(1)} %get-tuple-element.79.refs_0_, bf16[768,256]{1,0:T(8,128)(2,1)S(1)} %get-tuple-element.80.refs_1_.refs_0_, bf16[768,256]{1,0:T(8,128)(2,1)S(1)} %get-tuple-element.81.refs_2_.refs_1_, ...), custom_call_target="tpu_custom_call" | custom-call | tf_op jit(solution)/shard_map/intra_0/pallas_call | solution.py:54
  23.1 0.0 collective-permute-done.2.refs_0_
  23.2 1.2 %collective-permute-done.4.refs_2_ = bf16[2,128,128]{2,1,0:T(8,128)(2,1)S(1)} collective-permute-done((bf16[2,128,128]{2,1,0:T(8,128)(2,1)S(1)}, bf16[2,128,128]{2,1,0:T(8,128)(2,1)S(1)}, u32[]{:S(2)}, u32[]{:S(2)}) %collective-permute-start.4) | collective-permute-done | bytes 65568 | tf_op jit(solution)/shard_map/ppermute | solution.py:245
  24.4 0.2 pair_scan.1
  24.6 1.0 %collective-permute-start.5 = (bf16[2,2,128,128]{3,2,1,0:T(8,128)(2,1)S(1)}, bf16[2,2,128,128]{3,2,1,0:T(8,128)(2,1)S(1)}, u32[]{:S(2)}, u32[]{:S(2)}) collective-permute-start(bf16[2,2,128,128]{3,2,1,0:T(8,128)(2,1)S(1)} %get-tuple-element.86.refs_4_), channel_id=1, source_target_pairs={{0,32},{16,48},{32,0},{48,16},{64,96},{80,112},{96,64},{112,80},{1... | collective-permute-start | bytes 393224 | tf_op jit(solution)/shard_map/ppermute | solution.py:245
  25.6 2.5 %collective-permute-start.7 = (bf16[2,2,128,128]{3,2,1,0:T(8,128)(2,1)S(1)}, bf16[2,2,128,128]{3,2,1,0:T(8,128)(2,1)S(1)}, u32[]{:S(2)}, u32[]{:S(2)}) collective-permute-start(bf16[2,2,128,128]{3,2,1,0:T(8,128)(2,1)S(1)} %get-tuple-element.101), channel_id=1, source_target_pairs={{0,16},{16,0},{32,48},{48,32},{64,80},{80,64},{96,112},{112,96},{1... | collective-permute-start | bytes 393224 | tf_op jit(solution)/shard_map/ppermute | solution.py:245
  28.0 1.3 %final_0.1 = (bf16[768,1024]{1,0:T(8,128)(2,1)}, bf16[768,1024]{1,0:T(8,128)(2,1)}, bf16[768,1024]{1,0:T(8,128)(2,1)}, bf16[16,128]{1,0:T(8,128)(2,1)S(1)}) custom-call(bf16[768,256]{1,0:T(8,128)(2,1)S(1)} %get-tuple-element.80.refs_1_.refs_0_, bf16[768,256]{1,0:T(8,128)(2,1)S(1)} %get-tuple-element.81.refs_2_.refs_1_, ...), custom_call_target="tpu_custom_call" | custom-call | tf_op jit(solution)/shard_map/final_0/pallas_call | solution.py:54
  29.4 1.8 %intra_2.1 = (bf16[768,256]{1,0:T(8,128)(2,1)S(1)}, bf16[768,256]{1,0:T(8,128)(2,1)S(1)}, bf16[768,256]{1,0:T(8,128)(2,1)S(1)}) custom-call(bf16[768,256]{1,0:T(8,128)(2,1)S(1)} %get-tuple-element.90.refs_0_, bf16[768,256]{1,0:T(8,128)(2,1)S(1)} %get-tuple-element.91.refs_1_.refs_8_, bf16[768,256]{1,0:T(8,128)(2,1)S(1)} %get-tuple-element.92.refs_2_.refs_9_, ...), custom_call_target="tpu_custom_call" | custom-call | tf_op jit(solution)/shard_map/intra_2/pallas_call | solution.py:54
  31.2 0.1 near_scan.1
  31.3 0.1 collective-permute-start.6
  31.4 1.4 %final_1_2.1 = (bf16[16,128]{1,0:T(8,128)(2,1)}, bf16[768,256]{1,0:T(8,128)(2,1)S(1)}, bf16[768,256]{1,0:T(8,128)(2,1)S(1)}, bf16[768,256]{1,0:T(8,128)(2,1)S(1)...) custom-call(bf16[768,256]{1,0:T(8,128)(2,1)S(1)} %get-tuple-element.73.refs_1_.refs_0_, ...), custom_call_target="tpu_custom_call" | custom-call | tf_op jit(solution)/shard_map/final_1_2/pallas_call | solution.py:54
  32.8 2.6 %final_3.1 = (bf16[768,1024]{1,0:T(8,128)(2,1)}, bf16[768,1024]{1,0:T(8,128)(2,1)}, bf16[768,1024]{1,0:T(8,128)(2,1)}, bf16[16,128]{1,0:T(8,128)(2,1)}) custom-call(bf16[768,256]{1,0:T(8,128)(2,1)S(1)} %get-tuple-element.59.refs_1_.refs_0_, ...), custom_call_target="tpu_custom_call", output_to_operand_aliasing={{0}: (14, {}), {1}: (15, {}), {2}: (16, {})} | custom-call | tf_op jit(solution)/shard_map/final_3/pallas_call | solution.py:54
  (6 shorter events, 0.1 us)
Async XLA Ops:
  3.1 5.1 %collective-permute-start = (bf16[2,2,2,128,128]{4,3,2,1,0:T(8,128)(2,1)S(1)}, bf16[2,2,2,128,128]{4,3,2,1,0:T(8,128)(2,1)S(1)}, u32[]{:S(2)}, u32[]{:S(2)}) collective-permute-start(bf16[2,2,2,128,128]{4,3,2,1,0:T(8,128)(2,1)S(1)} %get-tuple-element.63.refs_4_), channel_id=1, source_target_pairs={{0,16},{16,0},{32,48},{48,32},{64,80},{80,64},{96,112},{112,96},{1... | collective-permute-start | bytes 786440 | tf_op jit(solution)/shard_map/ppermute | solution.py:245
  8.3 5.2 %collective-permute-start.1 = (bf16[2,2,128,128]{3,2,1,0:T(8,128)(2,1)S(1)}, bf16[2,2,128,128]{3,2,1,0:T(8,128)(2,1)S(1)}, u32[]{:S(2)}, u32[]{:S(2)}) collective-permute-start(bf16[2,2,128,128]{3,2,1,0:T(8,128)(2,1)S(1)} %fusion.refs_4_), channel_id=1, source_target_pairs={{0,32},{16,48},{32,0},{48,16},{64,96},{80,112},{96,64},{112,80},{1... | collective-permute-start | bytes 393224 | tf_op jit(solution)/shard_map/ppermute | solution.py:245
  13.5 9.6 %collective-permute-start.2 = (bf16[2,128,128]{2,1,0:T(8,128)(2,1)S(1)}, bf16[2,128,128]{2,1,0:T(8,128)(2,1)S(1)}, u32[]{:S(2)}, u32[]{:S(2)}) collective-permute-start(bf16[2,128,128]{2,1,0:T(8,128)(2,1)S(1)} %get-tuple-element.69.refs_4_), channel_id=1, source_target_pairs={{0,160},{16,176},{32,128},{48,144},{64,224},{80,240},{96,192},{112... | collective-permute-start | bytes 196616 | tf_op jit(solution)/shard_map/ppermute | solution.py:245
  18.4 4.8 %collective-permute-start.3 = (bf16[2,128,128]{2,1,0:T(8,128)(2,1)S(1)}, bf16[2,128,128]{2,1,0:T(8,128)(2,1)S(1)}, u32[]{:S(2)}, u32[]{:S(2)}) collective-permute-start(bf16[2,128,128]{2,1,0:T(8,128)(2,1)S(1)} %get-tuple-element.70), channel_id=1, source_target_pairs={{0,224},{16,240},{32,192},{48,208},{64,160},{80,176},{96,128},{112... | collective-permute-start | bytes 196616 | tf_op jit(solution)/shard_map/ppermute | solution.py:245
  18.4 6.0 %collective-permute-start.4 = (bf16[2,128,128]{2,1,0:T(8,128)(2,1)S(1)}, bf16[2,128,128]{2,1,0:T(8,128)(2,1)S(1)}, u32[]{:S(2)}, u32[]{:S(2)}) collective-permute-start(bf16[2,128,128]{2,1,0:T(8,128)(2,1)S(1)} %get-tuple-element.71), channel_id=1, source_target_pairs={{0,64},{16,80},{32,96},{48,112},{64,0},{80,16},{96,32},{112,48},{1... | collective-permute-start | bytes 196616 | tf_op jit(solution)/shard_map/ppermute | solution.py:245
  24.6 6.6 %collective-permute-start.5 = (bf16[2,2,128,128]{3,2,1,0:T(8,128)(2,1)S(1)}, bf16[2,2,128,128]{3,2,1,0:T(8,128)(2,1)S(1)}, u32[]{:S(2)}, u32[]{:S(2)}) collective-permute-start(bf16[2,2,128,128]{3,2,1,0:T(8,128)(2,1)S(1)} %get-tuple-element.86.refs_4_), channel_id=1, source_target_pairs={{0,32},{16,48},{32,0},{48,16},{64,96},{80,112},{96,64},{112,80},{1... | collective-permute-start | bytes 393224 | tf_op jit(solution)/shard_map/ppermute | solution.py:245
  25.6 5.8 %collective-permute-start.7 = (bf16[2,2,128,128]{3,2,1,0:T(8,128)(2,1)S(1)}, bf16[2,2,128,128]{3,2,1,0:T(8,128)(2,1)S(1)}, u32[]{:S(2)}, u32[]{:S(2)}) collective-permute-start(bf16[2,2,128,128]{3,2,1,0:T(8,128)(2,1)S(1)} %get-tuple-element.101), channel_id=1, source_target_pairs={{0,16},{16,0},{32,48},{48,32},{64,80},{80,64},{96,112},{112,96},{1... | collective-permute-start | bytes 393224 | tf_op jit(solution)/shard_map/ppermute | solution.py:245
  31.3 1.5 %collective-permute-start.6 = (bf16[2,2,128,128]{3,2,1,0:T(8,128)(2,1)S(1)}, bf16[2,2,128,128]{3,2,1,0:T(8,128)(2,1)S(1)}, u32[]{:S(2)}, u32[]{:S(2)}) collective-permute-start(bf16[2,2,128,128]{3,2,1,0:T(8,128)(2,1)S(1)} %get-tuple-element.97), channel_id=1, source_target_pairs={{0,16},{16,0},{32,48},{48,32},{64,80},{80,64},{96,112},{112,96},{1... | collective-permute-start | bytes 393224 | tf_op jit(solution)/shard_map/ppermute | solution.py:245

commit v5 on v4

--- a/solution.py
+++ b/solution.py
@@ -30,8 +30,8 @@
     return core, chip, low, quarter
 
 
-def pair_columns(core, quarter, pair):
-    of_core = core if pair < 2 else 1 - core
+def pair_columns(half, quarter, pair):
+    of_core = half if pair < 2 else 1 - half
     of_quarter = quarter if pair % 2 == 0 else 1 - quarter
     return pl.ds(pl.multiple_of((2 * of_core + of_quarter) * PAIR, PAIR), PAIR)
 
@@ -69,12 +69,13 @@
     results = refs[-5 * len(pairs) - 2 : -1]
     state_ref = results[0]
     sems = refs[-1]
-    core, _, _, quarter = places()
+    core, _, low, quarter = places()
+    half = lax.rem(core + low, 2)
     subs = sources[0].shape[0] // SUB
 
     def copy(step, which):
         return pltpu.make_async_copy(
-            sources[which].at[:, pair_columns(core, quarter, pairs[step])],
+            sources[which].at[:, pair_columns(half, quarter, pairs[step])],
             results[5 * step + 2 + which],
             sems.at[step, which],
         )
@@ -177,7 +178,8 @@
 def final_kernel(pairs, ready, keep, *refs):
     waiting = refs[8 * len(pairs) : 8 * len(pairs) + 3 * len(ready)]
     sems = refs[-1]
-    core, _, _, quarter = places()
+    core, _, low, quarter = places()
+    half = lax.rem(core + low, 2)
     copies = []
     count = 3 * len(pairs)
     if keep:
@@ -191,7 +193,7 @@
         rows = pl.ds(row, size)
         copy = pltpu.make_async_copy(
             buffer.at[rows],
-            outs[which].at[rows, pair_columns(core, quarter, pair)],
+            outs[which].at[rows, pair_columns(half, quarter, pair)],
             sems.at[len(copies)],
         )
         copy.start()
@@ -298,13 +300,13 @@
     core_10 = swap(state_32, 1)
     state_1, (local_1, held_1) = states((1,), state_32)
     sum_1 = (state_1[0].astype(F32) + core_10[0].astype(F32)).astype(BF16)
-    near_0 = swap(sum_1, 2)
+    near_0 = swap(sum_1, 3)
     state_0, (local_0, held_0) = states((0,), sum_1)
     partial_3 = intra(3, held_3, sum_1)
     sends = scan(
         pair_sum_kernel, "pair_sum", (state_0, core_10, near_0), partial_3, [(VMEM, (2,) + square)] * 3
     )
-    arrived = [swap(array, 2 * step) for step, array in zip(STEPS, sends)]
+    arrived = [swap(array, 2 * step + step % 2) for step, array in zip(STEPS, sends)]
     partial_1 = intra(1, held_1, sends[0])
     partial_0 = intra(0, held_0, sends[0])
     for_near, outer_0, wide_0 = scan(
@@ -314,7 +316,7 @@
         (*partial_1, *partial_0),
         [(VMEM, quarter)] * 3,
     )
-    from_near = swap(for_near, 2)
+    from_near = swap(for_near, 3)
     wide_2 = swap(outer_0, 1)
     partial_2 = intra(2, held_2, for_near)
     outs, token, _ = final({0: (held_0, partial_0, wide_0, local_0)}, ())

time: 35.7 us -> 36.5 us (1.022)
  waiting for transfers between devices: 2.74 us -> 4.4 us
  starting transfers between devices: 13.1 us -> 12.2 us
    ppermute x8, waiting for transfers between devices: 2.74 us -> 4.4 us  [swap(): return lax.ppermute(array, 'ctx', [(i, i ^ mask) for i in range(count_ctx)])]
    ppermute x8, starting transfers between devices: 13.1 us -> 12.2 us  [swap(): return lax.ppermute(array, 'ctx', [(i, i ^ mask) for i in range(count_ctx)])]
  transfers between devices with their start and end apart: 8 -> 8, of which waited for: 2 -> 4; matrix products, arithmetic and copies ran while one was open for 0% -> 0% of each run, Pallas kernels for 38% -> 37%
where the time goes in v5:
time: 36.5 us; the launch traced here: 36.3 us
  Pallas kernels  18.7 us (51%)
  starting transfers between devices  12.2 us (33%)
  waiting for transfers between devices  4.4 us (12%)
  between operations  0.91 us (2%)
    pallas_call x13, Pallas kernels, call(): pl.pallas_call(kernel, in_specs=[pl.BlockSpec(memory_space=space) for _,...  18.7 us
    ppermute x8, starting transfers between devices, swap(): return lax.ppermute(array, 'ctx', [(i, i ^ mask) for i in range(count_ctx)])  12.2 us
    ppermute x8, waiting for transfers between devices, swap(): return lax.ppermute(array, 'ctx', [(i, i ^ mask) for i in range(count_ctx)])  4.4 us
  transfers between devices with their start and end apart: 8, of which 4 were waited for; matrix products, arithmetic and copies ran while one was open for 0% of the time, Pallas kernels for 37%

profile of v5, /device:TPU:1, one launch (start us, length us, event | category | flops | bytes accessed | tf_op | source)
XLA Modules:
  0.0 36.3 jit_solution(16880794932931099968)
XLA Ops:
  0.6 2.5 %states_3_2.1 = (bf16[2,2,2,128,128]{4,3,2,1,0:T(8,128)(2,1)S(1)}, bf16[2,2,2,128,128]{4,3,2,1,0:T(8,128)(2,1)S(1)}, bf16[768,256]{1,0:T(8,128)(2,1)S(1)}, bf16[...) custom-call(bf16[768,1024]{1,0:T(8,128)(2,1)} %refs_0_.5, ...), custom_call_target="tpu_custom_call" | custom-call | tf_op jit(solution)/shard_map/states_3_2/pallas_call | solution.py:54
  3.1 3.3 %collective-permute-start = (bf16[2,2,2,128,128]{4,3,2,1,0:T(8,128)(2,1)S(1)}, bf16[2,2,2,128,128]{4,3,2,1,0:T(8,128)(2,1)S(1)}, u32[]{:S(2)}, u32[]{:S(2)}) collective-permute-start(bf16[2,2,2,128,128]{4,3,2,1,0:T(8,128)(2,1)S(1)} %get-tuple-element.63.refs_4_), channel_id=1, source_target_pairs={{0,16},{16,0},{32,48},{48,32},{64,80},{80,64},{96,112},{112,96},{1... | collective-permute-start | bytes 786440 | tf_op jit(solution)/shard_map/ppermute | solution.py:247
  6.4 1.8 %states_1.1 = (bf16[1,2,2,128,128]{4,3,2,1,0:T(8,128)(2,1)S(1)}, bf16[2,2,2,128,128]{4,3,2,1,0:T(8,128)(2,1)S(1)}, bf16[768,256]{1,0:T(8,128)(2,1)S(1)}, bf16[76...) custom-call(bf16[768,1024]{1,0:T(8,128)(2,1)} %refs_0_.5, ...), custom_call_target="tpu_custom_call" | custom-call | tf_op jit(solution)/shard_map/states_1/pallas_call | solution.py:54
  8.3 0.1 collective-permute-start.1
  8.4 1.8 %states_0.1 = (bf16[1,2,2,128,128]{4,3,2,1,0:T(8,128)(2,1)S(1)}, bf16[2,2,2,128,128]{4,3,2,1,0:T(8,128)(2,1)S(1)}, bf16[768,256]{1,0:T(8,128)(2,1)S(1)}, bf16[76...) custom-call(bf16[768,1024]{1,0:T(8,128)(2,1)} %refs_0_.5, ...), custom_call_target="tpu_custom_call" | custom-call | tf_op jit(solution)/shard_map/states_0/pallas_call | solution.py:54
  10.2 1.8 %intra_3.1 = (bf16[768,256]{1,0:T(8,128)(2,1)S(1)}, bf16[768,256]{1,0:T(8,128)(2,1)S(1)}, bf16[768,256]{1,0:T(8,128)(2,1)S(1)}) custom-call(bf16[768,256]{1,0:T(8,128)(2,1)S(1)} %get-tuple-element.62.refs_0_, bf16[768,256]{1,0:T(8,128)(2,1)S(1)} %get-tuple-element.59.refs_1_.refs_0_, bf16[768,256]{1,0:T(8,128)(2,1)S(1)} %get-tuple-element.60.refs_2_.refs_1_, ...), custom_call_target="tpu_custom_call" | custom-call | tf_op jit(solution)/shard_map/intra_3/pallas_call | solution.py:54
  12.0 1.6 %collective-permute-done.1.near_sum.refs_5_ = bf16[2,2,128,128]{3,2,1,0:T(8,128)(2,1)S(1)} collective-permute-done((bf16[2,2,128,128]{3,2,1,0:T(8,128)(2,1)S(1)}, bf16[2,2,128,128]{3,2,1,0:T(8,128)(2,1)S(1)}, u32[]{:S(2)}, u32[]{:S(2)}) %collective-permute-start.1) | collective-permute-done | bytes 131104 | tf_op jit(solution)/shard_map/ppermute | solution.py:247
  13.5 0.1 pair_sum.1
  13.6 4.8 %collective-permute-start.2 = (bf16[2,128,128]{2,1,0:T(8,128)(2,1)S(1)}, bf16[2,128,128]{2,1,0:T(8,128)(2,1)S(1)}, u32[]{:S(2)}, u32[]{:S(2)}) collective-permute-start(bf16[2,128,128]{2,1,0:T(8,128)(2,1)S(1)} %get-tuple-element.69.refs_4_), channel_id=1, source_target_pairs={{0,176},{16,160},{32,144},{48,128},{64,240},{80,224},{96,208},{112... | collective-permute-start | bytes 196616 | tf_op jit(solution)/shard_map/ppermute | solution.py:247
  18.4 1.3 %collective-permute-start.4 = (bf16[2,128,128]{2,1,0:T(8,128)(2,1)S(1)}, bf16[2,128,128]{2,1,0:T(8,128)(2,1)S(1)}, u32[]{:S(2)}, u32[]{:S(2)}) collective-permute-start(bf16[2,128,128]{2,1,0:T(8,128)(2,1)S(1)} %get-tuple-element.71), channel_id=1, source_target_pairs={{0,64},{16,80},{32,96},{48,112},{64,0},{80,16},{96,32},{112,48},{1... | collective-permute-start | bytes 196616 | tf_op jit(solution)/shard_map/ppermute | solution.py:247
  19.7 1.7 %intra_1.1 = (bf16[768,256]{1,0:T(8,128)(2,1)S(1)}, bf16[768,256]{1,0:T(8,128)(2,1)S(1)}, bf16[768,256]{1,0:T(8,128)(2,1)S(1)}) custom-call(bf16[768,256]{1,0:T(8,128)(2,1)S(1)} %get-tuple-element.72.refs_0_, bf16[768,256]{1,0:T(8,128)(2,1)S(1)} %get-tuple-element.73.refs_1_.refs_0_, bf16[768,256]{1,0:T(8,128)(2,1)S(1)} %get-tuple-element.74.refs_2_.refs_1_, ...), custom_call_target="tpu_custom_call" | custom-call | tf_op jit(solution)/shard_map/intra_1/pallas_call | solution.py:54
  21.4 1.7 %intra_0.1 = (bf16[768,256]{1,0:T(8,128)(2,1)S(1)}, bf16[768,256]{1,0:T(8,128)(2,1)S(1)}, bf16[768,256]{1,0:T(8,128)(2,1)S(1)}) custom-call(bf16[768,256]{1,0:T(8,128)(2,1)S(1)} %get-tuple-element.79.refs_0_, bf16[768,256]{1,0:T(8,128)(2,1)S(1)} %get-tuple-element.80.refs_1_.refs_0_, bf16[768,256]{1,0:T(8,128)(2,1)S(1)} %get-tuple-element.81.refs_2_.refs_1_, ...), custom_call_target="tpu_custom_call" | custom-call | tf_op jit(solution)/shard_map/intra_0/pallas_call | solution.py:54
  23.2 0.7 %collective-permute-done.3.refs_1_ = bf16[2,128,128]{2,1,0:T(8,128)(2,1)S(1)} collective-permute-done((bf16[2,128,128]{2,1,0:T(8,128)(2,1)S(1)}, bf16[2,128,128]{2,1,0:T(8,128)(2,1)S(1)}, u32[]{:S(2)}, u32[]{:S(2)}) %collective-permute-start.3) | collective-permute-done | bytes 65568 | tf_op jit(solution)/shard_map/ppermute | solution.py:247
  23.9 1.9 %collective-permute-done.4.refs_2_ = bf16[2,128,128]{2,1,0:T(8,128)(2,1)S(1)} collective-permute-done((bf16[2,128,128]{2,1,0:T(8,128)(2,1)S(1)}, bf16[2,128,128]{2,1,0:T(8,128)(2,1)S(1)}, u32[]{:S(2)}, u32[]{:S(2)}) %collective-permute-start.4) | collective-permute-done | bytes 65568 | tf_op jit(solution)/shard_map/ppermute | solution.py:247
  25.8 0.2 pair_scan.1
  26.0 2.3 %collective-permute-start.5 = (bf16[2,2,128,128]{3,2,1,0:T(8,128)(2,1)S(1)}, bf16[2,2,128,128]{3,2,1,0:T(8,128)(2,1)S(1)}, u32[]{:S(2)}, u32[]{:S(2)}) collective-permute-start(bf16[2,2,128,128]{3,2,1,0:T(8,128)(2,1)S(1)} %get-tuple-element.86.refs_4_), channel_id=1, source_target_pairs={{0,48},{16,32},{32,16},{48,0},{64,112},{80,96},{96,80},{112,64},{1... | collective-permute-start | bytes 393224 | tf_op jit(solution)/shard_map/ppermute | solution.py:247
  28.3 0.1 collective-permute-start.7
  28.4 1.3 %final_0.1 = (bf16[768,1024]{1,0:T(8,128)(2,1)}, bf16[768,1024]{1,0:T(8,128)(2,1)}, bf16[768,1024]{1,0:T(8,128)(2,1)}, bf16[16,128]{1,0:T(8,128)(2,1)S(1)}) custom-call(bf16[768,256]{1,0:T(8,128)(2,1)S(1)} %get-tuple-element.80.refs_1_.refs_0_, bf16[768,256]{1,0:T(8,128)(2,1)S(1)} %get-tuple-element.81.refs_2_.refs_1_, ...), custom_call_target="tpu_custom_call" | custom-call | tf_op jit(solution)/shard_map/final_0/pallas_call | solution.py:54
  29.8 1.8 %intra_2.1 = (bf16[768,256]{1,0:T(8,128)(2,1)S(1)}, bf16[768,256]{1,0:T(8,128)(2,1)S(1)}, bf16[768,256]{1,0:T(8,128)(2,1)S(1)}) custom-call(bf16[768,256]{1,0:T(8,128)(2,1)S(1)} %get-tuple-element.90.refs_0_, bf16[768,256]{1,0:T(8,128)(2,1)S(1)} %get-tuple-element.91.refs_1_.refs_8_, bf16[768,256]{1,0:T(8,128)(2,1)S(1)} %get-tuple-element.92.refs_2_.refs_9_, ...), custom_call_target="tpu_custom_call" | custom-call | tf_op jit(solution)/shard_map/intra_2/pallas_call | solution.py:54
  31.5 0.3 collective-permute-done.5.from_near
  31.8 0.1 near_scan.1
  31.9 0.3 collective-permute-start.6
  32.2 1.4 %final_1_2.1 = (bf16[16,128]{1,0:T(8,128)(2,1)}, bf16[768,256]{1,0:T(8,128)(2,1)S(1)}, bf16[768,256]{1,0:T(8,128)(2,1)S(1)}, bf16[768,256]{1,0:T(8,128)(2,1)S(1)...) custom-call(bf16[768,256]{1,0:T(8,128)(2,1)S(1)} %get-tuple-element.73.refs_1_.refs_0_, ...), custom_call_target="tpu_custom_call" | custom-call | tf_op jit(solution)/shard_map/final_1_2/pallas_call | solution.py:54
  33.6 2.6 %final_3.1 = (bf16[768,1024]{1,0:T(8,128)(2,1)}, bf16[768,1024]{1,0:T(8,128)(2,1)}, bf16[768,1024]{1,0:T(8,128)(2,1)}, bf16[16,128]{1,0:T(8,128)(2,1)}) custom-call(bf16[768,256]{1,0:T(8,128)(2,1)S(1)} %get-tuple-element.59.refs_1_.refs_0_, ...), custom_call_target="tpu_custom_call", output_to_operand_aliasing={{0}: (14, {}), {1}: (15, {}), {2}: (16, {})} | custom-call | tf_op jit(solution)/shard_map/final_3/pallas_call | solution.py:54
  (6 shorter events, 0.1 us)
Async XLA Ops:
  3.1 5.1 %collective-permute-start = (bf16[2,2,2,128,128]{4,3,2,1,0:T(8,128)(2,1)S(1)}, bf16[2,2,2,128,128]{4,3,2,1,0:T(8,128)(2,1)S(1)}, u32[]{:S(2)}, u32[]{:S(2)}) collective-permute-start(bf16[2,2,2,128,128]{4,3,2,1,0:T(8,128)(2,1)S(1)} %get-tuple-element.63.refs_4_), channel_id=1, source_target_pairs={{0,16},{16,0},{32,48},{48,32},{64,80},{80,64},{96,112},{112,96},{1... | collective-permute-start | bytes 786440 | tf_op jit(solution)/shard_map/ppermute | solution.py:247
  8.3 5.2 %collective-permute-start.1 = (bf16[2,2,128,128]{3,2,1,0:T(8,128)(2,1)S(1)}, bf16[2,2,128,128]{3,2,1,0:T(8,128)(2,1)S(1)}, u32[]{:S(2)}, u32[]{:S(2)}) collective-permute-start(bf16[2,2,128,128]{3,2,1,0:T(8,128)(2,1)S(1)} %fusion.refs_4_), channel_id=1, source_target_pairs={{0,48},{16,32},{32,16},{48,0},{64,112},{80,96},{96,80},{112,64},{1... | collective-permute-start | bytes 393224 | tf_op jit(solution)/shard_map/ppermute | solution.py:247
  13.6 9.6 %collective-permute-start.2 = (bf16[2,128,128]{2,1,0:T(8,128)(2,1)S(1)}, bf16[2,128,128]{2,1,0:T(8,128)(2,1)S(1)}, u32[]{:S(2)}, u32[]{:S(2)}) collective-permute-start(bf16[2,128,128]{2,1,0:T(8,128)(2,1)S(1)} %get-tuple-element.69.refs_4_), channel_id=1, source_target_pairs={{0,176},{16,160},{32,144},{48,128},{64,240},{80,224},{96,208},{112... | collective-permute-start | bytes 196616 | tf_op jit(solution)/shard_map/ppermute | solution.py:247
  18.4 5.5 %collective-permute-start.3 = (bf16[2,128,128]{2,1,0:T(8,128)(2,1)S(1)}, bf16[2,128,128]{2,1,0:T(8,128)(2,1)S(1)}, u32[]{:S(2)}, u32[]{:S(2)}) collective-permute-start(bf16[2,128,128]{2,1,0:T(8,128)(2,1)S(1)} %get-tuple-element.70), channel_id=1, source_target_pairs={{0,240},{16,224},{32,208},{48,192},{64,176},{80,160},{96,144},{112... | collective-permute-start | bytes 196616 | tf_op jit(solution)/shard_map/ppermute | solution.py:247
  18.4 7.4 %collective-permute-start.4 = (bf16[2,128,128]{2,1,0:T(8,128)(2,1)S(1)}, bf16[2,128,128]{2,1,0:T(8,128)(2,1)S(1)}, u32[]{:S(2)}, u32[]{:S(2)}) collective-permute-start(bf16[2,128,128]{2,1,0:T(8,128)(2,1)S(1)} %get-tuple-element.71), channel_id=1, source_target_pairs={{0,64},{16,80},{32,96},{48,112},{64,0},{80,16},{96,32},{112,48},{1... | collective-permute-start | bytes 196616 | tf_op jit(solution)/shard_map/ppermute | solution.py:247
  26.0 5.8 %collective-permute-start.5 = (bf16[2,2,128,128]{3,2,1,0:T(8,128)(2,1)S(1)}, bf16[2,2,128,128]{3,2,1,0:T(8,128)(2,1)S(1)}, u32[]{:S(2)}, u32[]{:S(2)}) collective-permute-start(bf16[2,2,128,128]{3,2,1,0:T(8,128)(2,1)S(1)} %get-tuple-element.86.refs_4_), channel_id=1, source_target_pairs={{0,48},{16,32},{32,16},{48,0},{64,112},{80,96},{96,80},{112,64},{1... | collective-permute-start | bytes 393224 | tf_op jit(solution)/shard_map/ppermute | solution.py:247
  28.3 3.9 %collective-permute-start.7 = (bf16[2,2,128,128]{3,2,1,0:T(8,128)(2,1)S(1)}, bf16[2,2,128,128]{3,2,1,0:T(8,128)(2,1)S(1)}, u32[]{:S(2)}, u32[]{:S(2)}) collective-permute-start(bf16[2,2,128,128]{3,2,1,0:T(8,128)(2,1)S(1)} %get-tuple-element.101), channel_id=1, source_target_pairs={{0,16},{16,0},{32,48},{48,32},{64,80},{80,64},{96,112},{112,96},{1... | collective-permute-start | bytes 393224 | tf_op jit(solution)/shard_map/ppermute | solution.py:247
  31.9 1.7 %collective-permute-start.6 = (bf16[2,2,128,128]{3,2,1,0:T(8,128)(2,1)S(1)}, bf16[2,2,128,128]{3,2,1,0:T(8,128)(2,1)S(1)}, u32[]{:S(2)}, u32[]{:S(2)}) collective-permute-start(bf16[2,2,128,128]{3,2,1,0:T(8,128)(2,1)S(1)} %get-tuple-element.97), channel_id=1, source_target_pairs={{0,16},{16,0},{32,48},{48,32},{64,80},{80,64},{96,112},{112,96},{1... | collective-permute-start | bytes 393224 | tf_op jit(solution)/shard_map/ppermute | solution.py:247

commit v6 on v4

--- a/solution.py
+++ b/solution.py
@@ -227,8 +227,10 @@
                 buffer[rows, :] = (
                     base[rows, :].astype(F32) + mm(rows_in[rows, :], weight, dims)
                 ).astype(BF16)
-                if not keep:
-                    send(buffer, pair, which, sub * SUB, SUB)
+                if not keep and sub == 0:
+                    send(buffer, pair, which, 0, SUB)
+                if not keep and sub == subs - 1:
+                    send(buffer, pair, which, SUB, (subs - 1) * SUB)
     for copy in copies:
         copy.wait()
 
@@ -279,7 +281,7 @@
         for arrays in ready.values():
             args += [(array, VMEM) for array in arrays]
         count = len(parts)
-        sends = 3 * len(ready) + (0 if keep else 3 * subs * count)
+        sends = 3 * len(ready) + (0 if keep else 6 * count)
         to_outs = [(pltpu.HBM, (rows, width))] * (3 if sends else 0)
         results = [(VMEM, held)] * 3 * count
         out = call(

time: 35.7 us -> 35.7 us (level)
  no operation moved by 1% of the time
where the time goes in v6:
time: 35.7 us; the launch traced here: 35.6 us
  Pallas kernels  18.8 us (53%)
  starting transfers between devices  13.1 us (37%)
  waiting for transfers between devices  2.74 us (8%)
  between operations  0.94 us (3%)
    pallas_call x13, Pallas kernels, call(): pl.pallas_call(kernel, in_specs=[pl.BlockSpec(memory_space=space) for _,...  18.8 us
    ppermute x8, starting transfers between devices, swap(): return lax.ppermute(array, 'ctx', [(i, i ^ mask) for i in range(count_ctx)])  13.1 us
    ppermute x8, waiting for transfers between devices, swap(): return lax.ppermute(array, 'ctx', [(i, i ^ mask) for i in range(count_ctx)])  2.74 us
  transfers between devices with their start and end apart: 8, of which 2 were waited for; matrix products, arithmetic and copies ran while one was open for 0% of the time, Pallas kernels for 38%

profile of v6, /device:TPU:1, one launch (start us, length us, event | category | flops | bytes accessed | tf_op | source)
XLA Modules:
  0.0 35.6 jit_solution(13657119473199995170)
XLA Ops:
  0.6 2.5 %states_3_2.1 = (bf16[2,2,2,128,128]{4,3,2,1,0:T(8,128)(2,1)S(1)}, bf16[2,2,2,128,128]{4,3,2,1,0:T(8,128)(2,1)S(1)}, bf16[768,256]{1,0:T(8,128)(2,1)S(1)}, bf16[...) custom-call(bf16[768,1024]{1,0:T(8,128)(2,1)} %refs_0_.5, ...), custom_call_target="tpu_custom_call" | custom-call | tf_op jit(solution)/shard_map/states_3_2/pallas_call | solution.py:54
  3.1 3.3 %collective-permute-start = (bf16[2,2,2,128,128]{4,3,2,1,0:T(8,128)(2,1)S(1)}, bf16[2,2,2,128,128]{4,3,2,1,0:T(8,128)(2,1)S(1)}, u32[]{:S(2)}, u32[]{:S(2)}) collective-permute-start(bf16[2,2,2,128,128]{4,3,2,1,0:T(8,128)(2,1)S(1)} %get-tuple-element.63.refs_4_), channel_id=1, source_target_pairs={{0,16},{16,0},{32,48},{48,32},{64,80},{80,64},{96,112},{112,96},{1... | collective-permute-start | bytes 786440 | tf_op jit(solution)/shard_map/ppermute | solution.py:247
  6.4 1.8 %states_1.1 = (bf16[1,2,2,128,128]{4,3,2,1,0:T(8,128)(2,1)S(1)}, bf16[2,2,2,128,128]{4,3,2,1,0:T(8,128)(2,1)S(1)}, bf16[768,256]{1,0:T(8,128)(2,1)S(1)}, bf16[76...) custom-call(bf16[768,1024]{1,0:T(8,128)(2,1)} %refs_0_.5, ...), custom_call_target="tpu_custom_call" | custom-call | tf_op jit(solution)/shard_map/states_1/pallas_call | solution.py:54
  8.2 0.0 collective-permute-done.core_ref.refs_4_
  8.3 0.1 collective-permute-start.1
  8.4 1.8 %states_0.1 = (bf16[1,2,2,128,128]{4,3,2,1,0:T(8,128)(2,1)S(1)}, bf16[2,2,2,128,128]{4,3,2,1,0:T(8,128)(2,1)S(1)}, bf16[768,256]{1,0:T(8,128)(2,1)S(1)}, bf16[76...) custom-call(bf16[768,1024]{1,0:T(8,128)(2,1)} %refs_0_.5, ...), custom_call_target="tpu_custom_call" | custom-call | tf_op jit(solution)/shard_map/states_0/pallas_call | solution.py:54
  10.2 1.8 %intra_3.1 = (bf16[768,256]{1,0:T(8,128)(2,1)S(1)}, bf16[768,256]{1,0:T(8,128)(2,1)S(1)}, bf16[768,256]{1,0:T(8,128)(2,1)S(1)}) custom-call(bf16[768,256]{1,0:T(8,128)(2,1)S(1)} %get-tuple-element.62.refs_0_, bf16[768,256]{1,0:T(8,128)(2,1)S(1)} %get-tuple-element.59.refs_1_.refs_0_, bf16[768,256]{1,0:T(8,128)(2,1)S(1)} %get-tuple-element.60.refs_2_.refs_1_, ...), custom_call_target="tpu_custom_call" | custom-call | tf_op jit(solution)/shard_map/intra_3/pallas_call | solution.py:54
  12.0 1.5 %collective-permute-done.1.near_sum.refs_5_ = bf16[2,2,128,128]{3,2,1,0:T(8,128)(2,1)S(1)} collective-permute-done((bf16[2,2,128,128]{3,2,1,0:T(8,128)(2,1)S(1)}, bf16[2,2,128,128]{3,2,1,0:T(8,128)(2,1)S(1)}, u32[]{:S(2)}, u32[]{:S(2)}) %collective-permute-start.1) | collective-permute-done | bytes 131104 | tf_op jit(solution)/shard_map/ppermute | solution.py:247
  13.5 0.1 pair_sum.1
  13.5 4.8 %collective-permute-start.2 = (bf16[2,128,128]{2,1,0:T(8,128)(2,1)S(1)}, bf16[2,128,128]{2,1,0:T(8,128)(2,1)S(1)}, u32[]{:S(2)}, u32[]{:S(2)}) collective-permute-start(bf16[2,128,128]{2,1,0:T(8,128)(2,1)S(1)} %get-tuple-element.69.refs_4_), channel_id=1, source_target_pairs={{0,160},{16,176},{32,128},{48,144},{64,224},{80,240},{96,192},{112... | collective-permute-start | bytes 196616 | tf_op jit(solution)/shard_map/ppermute | solution.py:247
  18.4 0.0 collective-permute-start.3
  18.4 1.3 %collective-permute-start.4 = (bf16[2,128,128]{2,1,0:T(8,128)(2,1)S(1)}, bf16[2,128,128]{2,1,0:T(8,128)(2,1)S(1)}, u32[]{:S(2)}, u32[]{:S(2)}) collective-permute-start(bf16[2,128,128]{2,1,0:T(8,128)(2,1)S(1)} %get-tuple-element.71), channel_id=1, source_target_pairs={{0,64},{16,80},{32,96},{48,112},{64,0},{80,16},{96,32},{112,48},{1... | collective-permute-start | bytes 196616 | tf_op jit(solution)/shard_map/ppermute | solution.py:247
  19.6 1.7 %intra_1.1 = (bf16[768,256]{1,0:T(8,128)(2,1)S(1)}, bf16[768,256]{1,0:T(8,128)(2,1)S(1)}, bf16[768,256]{1,0:T(8,128)(2,1)S(1)}) custom-call(bf16[768,256]{1,0:T(8,128)(2,1)S(1)} %get-tuple-element.72.refs_0_, bf16[768,256]{1,0:T(8,128)(2,1)S(1)} %get-tuple-element.73.refs_1_.refs_0_, bf16[768,256]{1,0:T(8,128)(2,1)S(1)} %get-tuple-element.74.refs_2_.refs_1_, ...), custom_call_target="tpu_custom_call" | custom-call | tf_op jit(solution)/shard_map/intra_1/pallas_call | solution.py:54
  21.4 1.7 %intra_0.1 = (bf16[768,256]{1,0:T(8,128)(2,1)S(1)}, bf16[768,256]{1,0:T(8,128)(2,1)S(1)}, bf16[768,256]{1,0:T(8,128)(2,1)S(1)}) custom-call(bf16[768,256]{1,0:T(8,128)(2,1)S(1)} %get-tuple-element.79.refs_0_, bf16[768,256]{1,0:T(8,128)(2,1)S(1)} %get-tuple-element.80.refs_1_.refs_0_, bf16[768,256]{1,0:T(8,128)(2,1)S(1)} %get-tuple-element.81.refs_2_.refs_1_, ...), custom_call_target="tpu_custom_call" | custom-call | tf_op jit(solution)/shard_map/intra_0/pallas_call | solution.py:54
  23.2 1.2 %collective-permute-done.4.refs_2_ = bf16[2,128,128]{2,1,0:T(8,128)(2,1)S(1)} collective-permute-done((bf16[2,128,128]{2,1,0:T(8,128)(2,1)S(1)}, bf16[2,128,128]{2,1,0:T(8,128)(2,1)S(1)}, u32[]{:S(2)}, u32[]{:S(2)}) %collective-permute-start.4) | collective-permute-done | bytes 65568 | tf_op jit(solution)/shard_map/ppermute | solution.py:247
  24.4 0.2 pair_scan.1
  24.6 1.0 %collective-permute-start.5 = (bf16[2,2,128,128]{3,2,1,0:T(8,128)(2,1)S(1)}, bf16[2,2,128,128]{3,2,1,0:T(8,128)(2,1)S(1)}, u32[]{:S(2)}, u32[]{:S(2)}) collective-permute-start(bf16[2,2,128,128]{3,2,1,0:T(8,128)(2,1)S(1)} %get-tuple-element.86.refs_4_), channel_id=1, source_target_pairs={{0,32},{16,48},{32,0},{48,16},{64,96},{80,112},{96,64},{112,80},{1... | collective-permute-start | bytes 393224 | tf_op jit(solution)/shard_map/ppermute | solution.py:247
  25.6 2.5 %collective-permute-start.7 = (bf16[2,2,128,128]{3,2,1,0:T(8,128)(2,1)S(1)}, bf16[2,2,128,128]{3,2,1,0:T(8,128)(2,1)S(1)}, u32[]{:S(2)}, u32[]{:S(2)}) collective-permute-start(bf16[2,2,128,128]{3,2,1,0:T(8,128)(2,1)S(1)} %get-tuple-element.101), channel_id=1, source_target_pairs={{0,16},{16,0},{32,48},{48,32},{64,80},{80,64},{96,112},{112,96},{1... | collective-permute-start | bytes 393224 | tf_op jit(solution)/shard_map/ppermute | solution.py:247
  28.0 1.4 %final_0.1 = (bf16[768,1024]{1,0:T(8,128)(2,1)}, bf16[768,1024]{1,0:T(8,128)(2,1)}, bf16[768,1024]{1,0:T(8,128)(2,1)}, bf16[16,128]{1,0:T(8,128)(2,1)S(1)}) custom-call(bf16[768,256]{1,0:T(8,128)(2,1)S(1)} %get-tuple-element.80.refs_1_.refs_0_, bf16[768,256]{1,0:T(8,128)(2,1)S(1)} %get-tuple-element.81.refs_2_.refs_1_, ...), custom_call_target="tpu_custom_call" | custom-call | tf_op jit(solution)/shard_map/final_0/pallas_call | solution.py:54
  29.5 1.8 %intra_2.1 = (bf16[768,256]{1,0:T(8,128)(2,1)S(1)}, bf16[768,256]{1,0:T(8,128)(2,1)S(1)}, bf16[768,256]{1,0:T(8,128)(2,1)S(1)}) custom-call(bf16[768,256]{1,0:T(8,128)(2,1)S(1)} %get-tuple-element.90.refs_0_, bf16[768,256]{1,0:T(8,128)(2,1)S(1)} %get-tuple-element.91.refs_1_.refs_8_, bf16[768,256]{1,0:T(8,128)(2,1)S(1)} %get-tuple-element.92.refs_2_.refs_9_, ...), custom_call_target="tpu_custom_call" | custom-call | tf_op jit(solution)/shard_map/intra_2/pallas_call | solution.py:54
  31.2 0.1 near_scan.1
  31.3 0.1 collective-permute-start.6
  31.4 1.4 %final_1_2.1 = (bf16[16,128]{1,0:T(8,128)(2,1)}, bf16[768,256]{1,0:T(8,128)(2,1)S(1)}, bf16[768,256]{1,0:T(8,128)(2,1)S(1)}, bf16[768,256]{1,0:T(8,128)(2,1)S(1)...) custom-call(bf16[768,256]{1,0:T(8,128)(2,1)S(1)} %get-tuple-element.73.refs_1_.refs_0_, ...), custom_call_target="tpu_custom_call" | custom-call | tf_op jit(solution)/shard_map/final_1_2/pallas_call | solution.py:54
  32.8 2.6 %final_3.1 = (bf16[768,1024]{1,0:T(8,128)(2,1)}, bf16[768,1024]{1,0:T(8,128)(2,1)}, bf16[768,1024]{1,0:T(8,128)(2,1)}, bf16[16,128]{1,0:T(8,128)(2,1)}) custom-call(bf16[768,256]{1,0:T(8,128)(2,1)S(1)} %get-tuple-element.59.refs_1_.refs_0_, ...), custom_call_target="tpu_custom_call", output_to_operand_aliasing={{0}: (14, {}), {1}: (15, {}), {2}: (16, {})} | custom-call | tf_op jit(solution)/shard_map/final_3/pallas_call | solution.py:54
  (6 shorter events, 0.1 us)
Async XLA Ops:
  3.1 5.1 %collective-permute-start = (bf16[2,2,2,128,128]{4,3,2,1,0:T(8,128)(2,1)S(1)}, bf16[2,2,2,128,128]{4,3,2,1,0:T(8,128)(2,1)S(1)}, u32[]{:S(2)}, u32[]{:S(2)}) collective-permute-start(bf16[2,2,2,128,128]{4,3,2,1,0:T(8,128)(2,1)S(1)} %get-tuple-element.63.refs_4_), channel_id=1, source_target_pairs={{0,16},{16,0},{32,48},{48,32},{64,80},{80,64},{96,112},{112,96},{1... | collective-permute-start | bytes 786440 | tf_op jit(solution)/shard_map/ppermute | solution.py:247
  8.3 5.2 %collective-permute-start.1 = (bf16[2,2,128,128]{3,2,1,0:T(8,128)(2,1)S(1)}, bf16[2,2,128,128]{3,2,1,0:T(8,128)(2,1)S(1)}, u32[]{:S(2)}, u32[]{:S(2)}) collective-permute-start(bf16[2,2,128,128]{3,2,1,0:T(8,128)(2,1)S(1)} %fusion.refs_4_), channel_id=1, source_target_pairs={{0,32},{16,48},{32,0},{48,16},{64,96},{80,112},{96,64},{112,80},{1... | collective-permute-start | bytes 393224 | tf_op jit(solution)/shard_map/ppermute | solution.py:247
  13.5 9.6 %collective-permute-start.2 = (bf16[2,128,128]{2,1,0:T(8,128)(2,1)S(1)}, bf16[2,128,128]{2,1,0:T(8,128)(2,1)S(1)}, u32[]{:S(2)}, u32[]{:S(2)}) collective-permute-start(bf16[2,128,128]{2,1,0:T(8,128)(2,1)S(1)} %get-tuple-element.69.refs_4_), channel_id=1, source_target_pairs={{0,160},{16,176},{32,128},{48,144},{64,224},{80,240},{96,192},{112... | collective-permute-start | bytes 196616 | tf_op jit(solution)/shard_map/ppermute | solution.py:247
  18.4 4.8 %collective-permute-start.3 = (bf16[2,128,128]{2,1,0:T(8,128)(2,1)S(1)}, bf16[2,128,128]{2,1,0:T(8,128)(2,1)S(1)}, u32[]{:S(2)}, u32[]{:S(2)}) collective-permute-start(bf16[2,128,128]{2,1,0:T(8,128)(2,1)S(1)} %get-tuple-element.70), channel_id=1, source_target_pairs={{0,224},{16,240},{32,192},{48,208},{64,160},{80,176},{96,128},{112... | collective-permute-start | bytes 196616 | tf_op jit(solution)/shard_map/ppermute | solution.py:247
  18.4 6.0 %collective-permute-start.4 = (bf16[2,128,128]{2,1,0:T(8,128)(2,1)S(1)}, bf16[2,128,128]{2,1,0:T(8,128)(2,1)S(1)}, u32[]{:S(2)}, u32[]{:S(2)}) collective-permute-start(bf16[2,128,128]{2,1,0:T(8,128)(2,1)S(1)} %get-tuple-element.71), channel_id=1, source_target_pairs={{0,64},{16,80},{32,96},{48,112},{64,0},{80,16},{96,32},{112,48},{1... | collective-permute-start | bytes 196616 | tf_op jit(solution)/shard_map/ppermute | solution.py:247
  24.6 6.6 %collective-permute-start.5 = (bf16[2,2,128,128]{3,2,1,0:T(8,128)(2,1)S(1)}, bf16[2,2,128,128]{3,2,1,0:T(8,128)(2,1)S(1)}, u32[]{:S(2)}, u32[]{:S(2)}) collective-permute-start(bf16[2,2,128,128]{3,2,1,0:T(8,128)(2,1)S(1)} %get-tuple-element.86.refs_4_), channel_id=1, source_target_pairs={{0,32},{16,48},{32,0},{48,16},{64,96},{80,112},{96,64},{112,80},{1... | collective-permute-start | bytes 393224 | tf_op jit(solution)/shard_map/ppermute | solution.py:247
  25.6 5.9 %collective-permute-start.7 = (bf16[2,2,128,128]{3,2,1,0:T(8,128)(2,1)S(1)}, bf16[2,2,128,128]{3,2,1,0:T(8,128)(2,1)S(1)}, u32[]{:S(2)}, u32[]{:S(2)}) collective-permute-start(bf16[2,2,128,128]{3,2,1,0:T(8,128)(2,1)S(1)} %get-tuple-element.101), channel_id=1, source_target_pairs={{0,16},{16,0},{32,48},{48,32},{64,80},{80,64},{96,112},{112,96},{1... | collective-permute-start | bytes 393224 | tf_op jit(solution)/shard_map/ppermute | solution.py:247
  31.3 1.5 %collective-permute-start.6 = (bf16[2,2,128,128]{3,2,1,0:T(8,128)(2,1)S(1)}, bf16[2,2,128,128]{3,2,1,0:T(8,128)(2,1)S(1)}, u32[]{:S(2)}, u32[]{:S(2)}) collective-permute-start(bf16[2,2,128,128]{3,2,1,0:T(8,128)(2,1)S(1)} %get-tuple-element.97), channel_id=1, source_target_pairs={{0,16},{16,0},{32,48},{48,32},{64,80},{80,64},{96,112},{112,96},{1... | collective-permute-start | bytes 393224 | tf_op jit(solution)/shard_map/ppermute | solution.py:247
